TPU v7x, 32 devices: a whole 2x2x4 slice. The times are simulated.
32 devices in a mesh: group: 4 (over y, x), strip: 8 (over z, core).
Axes of the slice: x: 2, y: 2, z: 4, core: 2. Of those that a mesh axis runs over, the one named last changes fastest.
Arguments:
- initial: float32 [4, 256, 1024], P('group', 'strip'), may hold values from -6 to 6
- conductivity: float32 [4, 256, 1024], P('group', 'strip'), may hold values from 0.5 to 1.5
- step_count: int32 [4], P('group'), may hold values from 16 to 32, as said below
- emit_steps: int32 [4, 16], P('group'), may hold values from 1 to 32
- assign: int32 [128], replicated, may hold values from 0 to 63
- sample_inputs: bfloat16 [128, 128], P(('group', 'strip')), may hold values from -6 to 6
- w_first: bfloat16 [128, 512], replicated, may hold values from -0.5 to 0.5
- w_second: bfloat16 [512, 512], replicated, may hold values from -0.25 to 0.25
- w_third: bfloat16 [512, 512], replicated, may hold values from -0.25 to 0.25
- w_out: bfloat16 [512, 256, 1024], P(None, 'strip', 'group'), may hold values from -0.25 to 0.25
Outputs:
- grad_first: float32 [128, 512], replicated
- grad_second: float32 [512, 512], replicated
- grad_third: float32 [512, 512], replicated
- grad_out: bfloat16 [512, 256, 1024], P(None, 'strip', 'group')
Inputs may be any that keep to these rules, and one draw needn't show every extreme that they name: `step_count`: at least 16; some field runs all 32 steps.
All inputs are finite; a program needn't handle non-finite values.
Results may differ from a plain program's by a relative error of at most 0.0039.
The roundings to bfloat16 on the way count: a program that leaves them out, or rounds other values in their place, can miss the bound.
Values may be sent and summed in bfloat16 or wider, within the bound.
No kernel may reach another device: no remote copies, remote signals or barrier semaphores. Data moves between devices by JAX's collectives and lax.ppermute only.
A program may use at most 64 MiB of HBM per device.

v0:
```python
import jax
import jax.numpy as jnp
from jax import lax
from jax.sharding import PartitionSpec as P

STEPS = 32


step_rate = 0.125


def padded(x, sides, width):
    for axis, dim in sides:
        count, length = (lax.axis_size(axis), x.shape[dim])
        up = [(i, (i + 1) % count) for i in range(count - 1)]
        down = [(j, i) for i, j in up]
        last = lax.slice_in_dim(x, length - width, length, axis=dim)
        initial = lax.slice_in_dim(x, 0, width, axis=dim)
        before = lax.ppermute(last, axis, up)
        after = lax.ppermute(initial, axis, down)
        x = jnp.concatenate([before, x, after], axis=dim)
    return x


def stencil(current, kappa_rows):
    middle = current[1:-1]
    zero_column = jnp.zeros((middle.shape[0], 1), jnp.float32)
    east_side = jnp.concatenate([middle[:, 1:], zero_column], axis=1)
    west_side = jnp.concatenate([zero_column, middle[:, :-1]], axis=1)
    beside_all = current[2:] + current[:-2] + east_side + west_side
    return middle + step_rate * kappa_rows * (1.0 + 0.25 * jnp.tanh(middle)) * (
        beside_all - 4.0 * middle
    )


def record(history, step_index, inner):
    return lax.dynamic_update_slice_in_dim(history, inner.astype(jnp.bfloat16)[None], step_index, 0)


def contract_rows(left, right):
    return lax.dot_general(
        left, right, (((0,), (0,)), ((), ())), preferred_element_type=jnp.float32
    )


def contract_cols(left, right):
    return lax.dot_general(
        left, right, (((1,), (1,)), ((), ())), preferred_element_type=jnp.float32
    )


def forward(inputs, w_first, w_second, w_third):
    act_a = jnp.tanh(jnp.dot(inputs, w_first, preferred_element_type=jnp.float32))
    hidden_a = act_a.astype(jnp.bfloat16)
    act_b = jnp.tanh(jnp.dot(hidden_a, w_second, preferred_element_type=jnp.float32))
    hidden_b = act_b.astype(jnp.bfloat16)
    act_c = jnp.tanh(jnp.dot(hidden_b, w_third, preferred_element_type=jnp.float32))
    hidden_c = act_c.astype(jnp.bfloat16)
    return ((act_a, act_b, act_c), (hidden_a, hidden_b, hidden_c))


def backward(inputs, activations, hiddens, w_second, w_third, back_c):
    delta_c = (back_c * (1.0 - activations[2] * activations[2])).astype(jnp.bfloat16)
    grad_third = contract_rows(hiddens[1], delta_c)
    back_b = contract_cols(delta_c, w_third)
    delta_b = (back_b * (1.0 - activations[1] * activations[1])).astype(jnp.bfloat16)
    grad_second = contract_rows(hiddens[0], delta_b)
    back_a = contract_cols(delta_b, w_second)
    delta_a = (back_a * (1.0 - activations[0] * activations[0])).astype(jnp.bfloat16)
    grad_first = contract_rows(inputs, delta_a)
    return (grad_first, grad_second, grad_third)


def per_device(
    initial,
    conductivity,
    step_count,
    emit_steps,
    assign,
    sample_inputs,
    w_first,
    w_second,
    w_third,
    w_out,
):
    field_now = initial[0]
    kappa = conductivity[0]
    run_steps = step_count[0]
    emit_row = emit_steps[0]
    row_count = field_now.shape[0]
    start_history = jnp.zeros((STEPS, row_count, field_now.shape[1]), jnp.bfloat16)
    halo_width = 4
    kappa_wide = padded(kappa, (("strip", 0),), halo_width)
    first_row = lax.axis_index("strip") * row_count - halo_width
    global_rows = first_row + jnp.arange(row_count + 2 * halo_width, dtype=jnp.int32)
    inside = ((global_rows >= 0) & (global_rows < row_count * lax.axis_size("strip"))).astype(
        jnp.float32
    )[:, None]

    def block_steps(block_index, carried):
        current, history = carried
        widened = padded(current, (("strip", 0),), halo_width)
        for substep in range(halo_width):
            step_index = block_index * halo_width + substep
            low_row = substep + 1
            span_rows = row_count + 2 * (halo_width - substep - 1)
            candidate = (
                stencil(widened, kappa_wide[low_row : low_row + span_rows])
                * inside[low_row : low_row + span_rows]
            )
            widened = jnp.where(step_index < run_steps, candidate, widened[1:-1])
            offset = halo_width - substep - 1
            history = record(history, step_index, widened[offset : offset + row_count])
        return (widened, history)

    field_now, history = lax.fori_loop(
        0, STEPS // halo_width, block_steps, (field_now, start_history)
    )
    snapshots = jnp.take(history, emit_row - 1, axis=0)
    regrouped = lax.all_to_all(snapshots[None], "group", split_axis=3, concat_axis=0, tiled=True)
    flat_snaps = regrouped.reshape(regrouped.shape[0] * regrouped.shape[1], -1)
    targets = jnp.take(flat_snaps, assign, axis=0)
    weight_flat = w_out.reshape(w_out.shape[0], -1)
    inverse_root = 1.0 / jnp.sqrt(jnp.float32(assign.shape[0]))
    activations, hiddens = forward(sample_inputs, w_first, w_second, w_third)
    hidden_all = lax.all_gather(hiddens[2], ("group", "strip"), axis=0, tiled=True)
    predicted = jnp.dot(hidden_all, weight_flat, preferred_element_type=jnp.float32)
    output_residual = ((predicted - targets.astype(jnp.float32)) * inverse_root).astype(
        jnp.bfloat16
    )
    grad_out = contract_rows(hidden_all, output_residual).astype(jnp.bfloat16)
    residual, grad_out = (output_residual, grad_out)
    back_c = lax.psum_scatter(
        contract_cols(residual, weight_flat), ("group", "strip"), scatter_dimension=0, tiled=True
    )
    partial_grads = backward(sample_inputs, activations, hiddens, w_second, w_third, back_c)
    grad_first, grad_second, grad_third = lax.psum(
        (partial_grads[0], partial_grads[1], partial_grads[2]), ("group", "strip")
    )
    return (grad_first, grad_second, grad_third, grad_out.reshape(w_out.shape))


def solution(mesh):
    placed = (
        P("group", "strip", None),
        P("group", "strip", None),
        P("group"),
        P("group", None),
        P(),
        P(("group", "strip"), None),
        P(),
        P(),
        P(),
        P(None, "strip", "group"),
    )
    return jax.shard_map(
        per_device,
        mesh=mesh,
        in_specs=placed,
        out_specs=(P(), P(), P(), P(None, "strip", "group")),
        check_vma=False,
    )
```

profile of v0, /device:TPU:0, one launch (start us, length us, event | category | flops | bytes accessed | tf_op | source)
XLA Modules:
  0.0 474.1 jit_solution(13398654894622168346)
XLA Ops:
  8.1 2.3 collective-permute-start.2
  16.9 78.9 %while.17 = (s32[]{:T(128)}, f32[32,1024]{1,0:T(8,128)S(1)}, bf16[32,32,1024]{2,1,0:T(8,128)(2,1)S(1)}, s32[]{:T(128)}, f32[40,1024]{1,0:T(8,128)S(1)}, /*index=...) while((s32[]{:T(128)}, f32[32,1024]{1,0:T(8,128)S(1)}, ...), condition=%wide.region_1.2_spmd, body=%wide.region_0.1_spmd.sunk | while | flops 1978390 | bytes 7290309 | solution.py:116
  18.2 5.7 %collective-permute-start.1 = (f32[4,1024]{1,0:T(4,128)S(1)}, f32[4,1024]{1,0:T(4,128)S(1)}, u32[]{:S(2)}, u32[]{:S(2)}) collective-permute-start(f32[4,1024]{1,0:T(4,128)S(1)} %get-tuple-element.282), channel_id=1, source_target_pairs={{0,1},{1,2},{2,3},{3,4},{4,5},{5,6},{6,7},{8,9},{9,10},{10,11},{11... | collective-permute-start | bytes 49160 | tf_op jit(solution)/shard_map/while/body/eval_jaxpr/ppermute | solution.py:19
  29.4 4.3 collective-permute-start.1
  39.0 4.3 collective-permute-start.1
  48.7 4.3 collective-permute-start.1
  58.4 4.3 collective-permute-start.1
  68.1 4.3 collective-permute-start.1
  77.8 4.3 collective-permute-start.1
  87.4 4.3 collective-permute-start.1
  98.8 4.7 copy.18
  103.5 6.4 %reshape.112 = bf16[4,2,65536]{2,1,0:T(2,128)(2,1)} reshape(bf16[1024,1,16,32]{3,2,1,0:T(8,128)(2,1)} %bitcast.92) | data formatting | bytes 2097152
  109.9 3.7 all-to-all-start
  113.6 43.4 %all-gather = bf16[32,4,512]{2,1,0:T(4,128)(2,1)S(1)} all-gather(bf16[1,4,512]{2,1,0:T(4,128)(2,1)S(1)} %convert_bitcast_fusion), channel_id=1, replica_groups=mesh['group'=4,'strip'=8] {'group','strip'}, dimensions={0}, use_global_device_ids=true | all-gather | bytes 135168 | tf_op jit(solution)/shard_map/all_gather | solution.py:126
  157.1 16.6 %copy.21 = bf16[64,8,32,256]{3,1,2,0:T(8,128)(2,1)} copy(bf16[64,8,32,256]{3,2,1,0:T(8,128)(2,1)} %bitcast.94) | data formatting | bytes 16777216
  173.8 3.7 reshape.113
  177.5 4.8 %copy.19 = bf16[1,16,32,4,256]{4,2,1,3,0:T(8,128)(2,1)S(1)} copy(bf16[1,16,32,4,256]{2,1,4,3,0:T(8,128)(2,1)} %bitcast.93) | data formatting | bytes 2097152 | tf_op jit(solution)/shard_map/all_to_all | solution.py:120
  182.9 3.2 gather_fusion.1
  186.1 5.7 %fusion.35 = bf16[128,8192]{1,0:T(8,128)(2,1)S(1)} fusion(bf16[128,512]{1,0:T(8,128)(2,1)S(1)} %reshape.111, bf16[512,8192]{1,0:T(8,128)(2,1)} %bitcast.89, bf16[128,8192]{1,0:T(8,128)(2,1)} %gather_fusion.1, pred[128]{0:T(512)(128)(4,1)S(1)} %compare_and_fusion.1), kind=kOutput, calls=%fused_computation.52 | convolution fusion | flops 1078984704 | bytes 12714112 | tf_op jit(solution)/shard_map/dot_general | solution.py:127
  191.8 7.1 %fusion.58 = f32[128,512]{1,0:T(8,128)} fusion(bf16[128,8192]{1,0:T(8,128)(2,1)S(1)} %fusion.35, bf16[512,8192]{1,0:T(8,128)(2,1)} %bitcast.90), kind=kOutput, calls=%fused_computation.92 | convolution fusion | flops 1073741824 | bytes 10747904 | tf_op jit(solution)/shard_map/dot_general | solution.py:47
  199.2 121.1 %all-reduce.13.cloned.1.call-done = f32[128,512]{1,0:T(8,128)} async-done(((f32[128,512]{1,0:T(8,128)}), f32[128,512]{1,0:T(8,128)}) %all-reduce.13.cloned.1.call-update) | async-done | bytes 262160
  325.9 5.6 %convolution_convert_fusion = bf16[512,8192]{1,0:T(8,128)(2,1)} fusion(bf16[128,512]{1,0:T(8,128)(2,1)S(1)} %reshape.111, bf16[128,8192]{1,0:T(8,128)(2,1)S(1)} %fusion.35), kind=kOutput, calls=%fused_computation.49 | convolution fusion | flops 1077936128 | bytes 10616832 | tf_op jit(solution)/shard_map/dot_general | solution.py:41
  331.6 9.7 %copy.23 = bf16[64,8,32,256]{3,2,1,0:T(8,128)(2,1)} copy(bf16[64,8,32,256]{3,1,2,0:T(8,128)(2,1)} %bitcast.91) | data formatting | bytes 16777216
  341.3 120.8 %all-reduce.15.cloned.1.call-done = (f32[128,512]{0,1:T(8,128)}, f32[512,512]{1,0:T(8,128)}, f32[512,512]{1,0:T(8,128)}) async-done(((f32[128,512]{0,1:T(8,128)}, f32[512,512]{1,0:T(8,128)}, f32[512,512]{1,0:T(8,128)}), (f32[128,512]{0,1:T(8,128)}, f32[512,512]{1,0:T(8,128)}, f32[512,512]{1,0:T(8,128)})) %all-reduce.15.cloned.1.call-update) | async-done | bytes 2359312 | tf_op jit(solution)/shard_map/psum | solution.py:137
  (207 shorter events, 43.2 us)
Async XLA Ops:
  8.1 7.5 %collective-permute-start.2 = (f32[4,1024]{1,0:T(4,128)S(1)}, f32[4,1024]{1,0:T(4,128)S(1)}, u32[]{:S(2)}, u32[]{:S(2)}) collective-permute-start(f32[4,1024]{1,0:T(4,128)S(1)} %get-tuple-element.224), channel_id=1, source_target_pairs={{0,1},{1,2},{2,3},{3,4},{4,5},{5,6},{6,7},{8,9},{9,10},{10,11},{11... | collective-permute-start | bytes 49160 | tf_op jit(solution)/shard_map/ppermute | solution.py:19
  10.4 5.3 %collective-permute-start.3 = (f32[4,1024]{1,0:T(4,128)S(1)}, f32[4,1024]{1,0:T(4,128)S(1)}, u32[]{:S(2)}, u32[]{:S(2)}) collective-permute-start(f32[4,1024]{1,0:T(4,128)S(1)} %get-tuple-element.225), channel_id=1, source_target_pairs={{1,0},{2,1},{3,2},{4,3},{5,4},{6,5},{7,6},{9,8},{10,9},{11,10},{12... | collective-permute-start | bytes 49160 | tf_op jit(solution)/shard_map/ppermute | solution.py:20
  16.9 9.9 %collective-permute-start = (f32[4,1024]{1,0:T(4,128)S(1)}, f32[4,1024]{1,0:T(4,128)S(1)}, u32[]{:S(2)}, u32[]{:S(2)}) collective-permute-start(f32[4,1024]{1,0:T(4,128)S(1)} %get-tuple-element.281), channel_id=1, source_target_pairs={{1,0},{2,1},{3,2},{4,3},{5,4},{6,5},{7,6},{9,8},{10,9},{11,10},{12... | collective-permute-start | bytes 49160 | tf_op jit(solution)/shard_map/while/body/eval_jaxpr/ppermute | solution.py:20
  18.2 8.6 %collective-permute-start.1 = (f32[4,1024]{1,0:T(4,128)S(1)}, f32[4,1024]{1,0:T(4,128)S(1)}, u32[]{:S(2)}, u32[]{:S(2)}) collective-permute-start(f32[4,1024]{1,0:T(4,128)S(1)} %get-tuple-element.282), channel_id=1, source_target_pairs={{0,1},{1,2},{2,3},{3,4},{4,5},{5,6},{6,7},{8,9},{9,10},{10,11},{11... | collective-permute-start | bytes 49160 | tf_op jit(solution)/shard_map/while/body/eval_jaxpr/ppermute | solution.py:19
  28.1 8.5 %collective-permute-start = (f32[4,1024]{1,0:T(4,128)S(1)}, f32[4,1024]{1,0:T(4,128)S(1)}, u32[]{:S(2)}, u32[]{:S(2)}) collective-permute-start(f32[4,1024]{1,0:T(4,128)S(1)} %get-tuple-element.281), channel_id=1, source_target_pairs={{1,0},{2,1},{3,2},{4,3},{5,4},{6,5},{7,6},{9,8},{10,9},{11,10},{12... | collective-permute-start | bytes 49160 | tf_op jit(solution)/shard_map/while/body/eval_jaxpr/ppermute | solution.py:20
  29.4 7.2 %collective-permute-start.1 = (f32[4,1024]{1,0:T(4,128)S(1)}, f32[4,1024]{1,0:T(4,128)S(1)}, u32[]{:S(2)}, u32[]{:S(2)}) collective-permute-start(f32[4,1024]{1,0:T(4,128)S(1)} %get-tuple-element.282), channel_id=1, source_target_pairs={{0,1},{1,2},{2,3},{3,4},{4,5},{5,6},{6,7},{8,9},{9,10},{10,11},{11... | collective-permute-start | bytes 49160 | tf_op jit(solution)/shard_map/while/body/eval_jaxpr/ppermute | solution.py:19
  37.7 8.5 %collective-permute-start = (f32[4,1024]{1,0:T(4,128)S(1)}, f32[4,1024]{1,0:T(4,128)S(1)}, u32[]{:S(2)}, u32[]{:S(2)}) collective-permute-start(f32[4,1024]{1,0:T(4,128)S(1)} %get-tuple-element.281), channel_id=1, source_target_pairs={{1,0},{2,1},{3,2},{4,3},{5,4},{6,5},{7,6},{9,8},{10,9},{11,10},{12... | collective-permute-start | bytes 49160 | tf_op jit(solution)/shard_map/while/body/eval_jaxpr/ppermute | solution.py:20
  39.0 7.2 %collective-permute-start.1 = (f32[4,1024]{1,0:T(4,128)S(1)}, f32[4,1024]{1,0:T(4,128)S(1)}, u32[]{:S(2)}, u32[]{:S(2)}) collective-permute-start(f32[4,1024]{1,0:T(4,128)S(1)} %get-tuple-element.282), channel_id=1, source_target_pairs={{0,1},{1,2},{2,3},{3,4},{4,5},{5,6},{6,7},{8,9},{9,10},{10,11},{11... | collective-permute-start | bytes 49160 | tf_op jit(solution)/shard_map/while/body/eval_jaxpr/ppermute | solution.py:19
  47.4 8.5 %collective-permute-start = (f32[4,1024]{1,0:T(4,128)S(1)}, f32[4,1024]{1,0:T(4,128)S(1)}, u32[]{:S(2)}, u32[]{:S(2)}) collective-permute-start(f32[4,1024]{1,0:T(4,128)S(1)} %get-tuple-element.281), channel_id=1, source_target_pairs={{1,0},{2,1},{3,2},{4,3},{5,4},{6,5},{7,6},{9,8},{10,9},{11,10},{12... | collective-permute-start | bytes 49160 | tf_op jit(solution)/shard_map/while/body/eval_jaxpr/ppermute | solution.py:20
  48.7 7.2 %collective-permute-start.1 = (f32[4,1024]{1,0:T(4,128)S(1)}, f32[4,1024]{1,0:T(4,128)S(1)}, u32[]{:S(2)}, u32[]{:S(2)}) collective-permute-start(f32[4,1024]{1,0:T(4,128)S(1)} %get-tuple-element.282), channel_id=1, source_target_pairs={{0,1},{1,2},{2,3},{3,4},{4,5},{5,6},{6,7},{8,9},{9,10},{10,11},{11... | collective-permute-start | bytes 49160 | tf_op jit(solution)/shard_map/while/body/eval_jaxpr/ppermute | solution.py:19
  57.1 8.5 %collective-permute-start = (f32[4,1024]{1,0:T(4,128)S(1)}, f32[4,1024]{1,0:T(4,128)S(1)}, u32[]{:S(2)}, u32[]{:S(2)}) collective-permute-start(f32[4,1024]{1,0:T(4,128)S(1)} %get-tuple-element.281), channel_id=1, source_target_pairs={{1,0},{2,1},{3,2},{4,3},{5,4},{6,5},{7,6},{9,8},{10,9},{11,10},{12... | collective-permute-start | bytes 49160 | tf_op jit(solution)/shard_map/while/body/eval_jaxpr/ppermute | solution.py:20
  58.4 7.2 %collective-permute-start.1 = (f32[4,1024]{1,0:T(4,128)S(1)}, f32[4,1024]{1,0:T(4,128)S(1)}, u32[]{:S(2)}, u32[]{:S(2)}) collective-permute-start(f32[4,1024]{1,0:T(4,128)S(1)} %get-tuple-element.282), channel_id=1, source_target_pairs={{0,1},{1,2},{2,3},{3,4},{4,5},{5,6},{6,7},{8,9},{9,10},{10,11},{11... | collective-permute-start | bytes 49160 | tf_op jit(solution)/shard_map/while/body/eval_jaxpr/ppermute | solution.py:19
  66.8 8.5 %collective-permute-start = (f32[4,1024]{1,0:T(4,128)S(1)}, f32[4,1024]{1,0:T(4,128)S(1)}, u32[]{:S(2)}, u32[]{:S(2)}) collective-permute-start(f32[4,1024]{1,0:T(4,128)S(1)} %get-tuple-element.281), channel_id=1, source_target_pairs={{1,0},{2,1},{3,2},{4,3},{5,4},{6,5},{7,6},{9,8},{10,9},{11,10},{12... | collective-permute-start | bytes 49160 | tf_op jit(solution)/shard_map/while/body/eval_jaxpr/ppermute | solution.py:20
  68.1 7.2 %collective-permute-start.1 = (f32[4,1024]{1,0:T(4,128)S(1)}, f32[4,1024]{1,0:T(4,128)S(1)}, u32[]{:S(2)}, u32[]{:S(2)}) collective-permute-start(f32[4,1024]{1,0:T(4,128)S(1)} %get-tuple-element.282), channel_id=1, source_target_pairs={{0,1},{1,2},{2,3},{3,4},{4,5},{5,6},{6,7},{8,9},{9,10},{10,11},{11... | collective-permute-start | bytes 49160 | tf_op jit(solution)/shard_map/while/body/eval_jaxpr/ppermute | solution.py:19
  76.5 8.5 %collective-permute-start = (f32[4,1024]{1,0:T(4,128)S(1)}, f32[4,1024]{1,0:T(4,128)S(1)}, u32[]{:S(2)}, u32[]{:S(2)}) collective-permute-start(f32[4,1024]{1,0:T(4,128)S(1)} %get-tuple-element.281), channel_id=1, source_target_pairs={{1,0},{2,1},{3,2},{4,3},{5,4},{6,5},{7,6},{9,8},{10,9},{11,10},{12... | collective-permute-start | bytes 49160 | tf_op jit(solution)/shard_map/while/body/eval_jaxpr/ppermute | solution.py:20
  77.8 7.2 %collective-permute-start.1 = (f32[4,1024]{1,0:T(4,128)S(1)}, f32[4,1024]{1,0:T(4,128)S(1)}, u32[]{:S(2)}, u32[]{:S(2)}) collective-permute-start(f32[4,1024]{1,0:T(4,128)S(1)} %get-tuple-element.282), channel_id=1, source_target_pairs={{0,1},{1,2},{2,3},{3,4},{4,5},{5,6},{6,7},{8,9},{9,10},{10,11},{11... | collective-permute-start | bytes 49160 | tf_op jit(solution)/shard_map/while/body/eval_jaxpr/ppermute | solution.py:19
  86.1 8.5 %collective-permute-start = (f32[4,1024]{1,0:T(4,128)S(1)}, f32[4,1024]{1,0:T(4,128)S(1)}, u32[]{:S(2)}, u32[]{:S(2)}) collective-permute-start(f32[4,1024]{1,0:T(4,128)S(1)} %get-tuple-element.281), channel_id=1, source_target_pairs={{1,0},{2,1},{3,2},{4,3},{5,4},{6,5},{7,6},{9,8},{10,9},{11,10},{12... | collective-permute-start | bytes 49160 | tf_op jit(solution)/shard_map/while/body/eval_jaxpr/ppermute | solution.py:20
  87.4 7.2 %collective-permute-start.1 = (f32[4,1024]{1,0:T(4,128)S(1)}, f32[4,1024]{1,0:T(4,128)S(1)}, u32[]{:S(2)}, u32[]{:S(2)}) collective-permute-start(f32[4,1024]{1,0:T(4,128)S(1)} %get-tuple-element.282), channel_id=1, source_target_pairs={{0,1},{1,2},{2,3},{3,4},{4,5},{5,6},{6,7},{8,9},{9,10},{10,11},{11... | collective-permute-start | bytes 49160 | tf_op jit(solution)/shard_map/while/body/eval_jaxpr/ppermute | solution.py:19
  109.9 63.9 %all-to-all-start = ((bf16[4,2,65536]{2,1,0:T(2,128)(2,1)}), bf16[4,2,65536]{2,1,0:T(2,128)(2,1)S(1)}, u32[]{:S(2)}, u32[]{:S(2)}) async-start(bf16[4,2,65536]{2,1,0:T(2,128)(2,1)} %reshape.112), calls=%async_computation | async-start | bytes 2097152 | tf_op jit(solution)/shard_map/all_to_all | solution.py:120
  113.6 206.8 %all-reduce.13.cloned.1.call-start = ((), (), s32[]{:S(2)}) async-start(), calls=%async_computation.1 | async-start | bytes 524288
  157.1 16.6 %copy-start.6 = (s32[128]{0:T(128)S(1)}, s32[128]{0:T(128)}, u32[]{:S(2)}) copy-start(s32[128]{0:T(128)} %param.16) | copy-start | bytes 1540
  191.8 128.6 %copy-start.3 = (bf16[512,512]{1,0:T(8,128)(2,1)S(1)}, bf16[512,512]{1,0:T(8,128)(2,1)}, u32[]{:S(2)}) copy-start(bf16[512,512]{1,0:T(8,128)(2,1)} %param.20) | copy-start | bytes 1572868
  191.8 129.5 %copy-start.5 = (bf16[4,128]{1,0:T(4,128)(2,1)S(1)}, bf16[4,128]{1,0:T(4,128)(2,1)}, u32[]{:S(2)}) copy-start(bf16[4,128]{1,0:T(4,128)(2,1)} %param.17) | copy-start | bytes 3076
  198.9 263.2 %all-reduce.15.cloned.1.call-start = ((), (), s32[]{:S(2)}) async-start(), calls=%async_computation.2 | async-start | bytes 4718592 | tf_op jit(solution)/shard_map/psum | solution.py:137
  (4 other events, 30.4 us)
Sparse Core Ops, SparseCore 0:
  199.0 121.2 all-reduce.12
  326.8 135.2 all-reduce.14
where the time goes:
time: 476 us; the launch traced here: 474 us
  waiting for transfers between devices  242 us (51%)
  local copies, waits for them, and re-layouts  63.8 us (13%)
  starting transfers between devices  53.6 us (11%)
  blocking collectives  43.4 us (9%)
  matrix products  26.3 us (6%)
  loops' own time  22 us (5%)
  between operations  14.2 us (3%)
  other arithmetic  8.46 us (2%)
    unnamed x3, waiting for transfers between devices  121 us
    psum x1, waiting for transfers between devices, per_device(): lax.psum((partial_grads[0], partial_grads[1], partial_grads[2]), ('group'...  121 us
    all_gather x1, blocking collectives, per_device(): lax.all_gather(hiddens[2], ('group', 'strip'), axis=0, tiled=True)  43.4 us
    unnamed x23, local copies, waits for them, and re-layouts  42.3 us
    ppermute x9, starting transfers between devices, padded(): before = lax.ppermute(last, axis, up)  38 us
    another operation x1, loops' own time, per_device(): lax.fori_loop(0, STEPS // halo_width, block_steps, (field_now, start_hist...  22 us
    ppermute x9, starting transfers between devices, padded(): after = lax.ppermute(initial, axis, down)  11.6 us
    dot_general x4, matrix products, contract_rows(): lax.dot_general(left, right, (((0,), (0,)), ((), ())), preferred_element_...  10.2 us
  transfers between devices with their start and end apart: 21, of which 3 were waited for; matrix products, arithmetic and copies ran while one was open for 8% of the time, Pallas kernels for 0%

commit v1 on v0

v1 whole, which is shorter than its diff:
```python
import functools

import jax
import jax.numpy as jnp
from jax import lax
from jax.experimental import pallas as pl
from jax.experimental.pallas import tpu as pltpu
from jax.sharding import PartitionSpec as P

STEPS = 32
LANES = 128
step_rate = 0.125

BF16 = jnp.bfloat16
F32 = jnp.float32
ALL = ("group", "strip")
whole = pl.BlockSpec(memory_space=pltpu.VMEM)
scalars = pl.BlockSpec(memory_space=pltpu.SMEM)


def params(mebibytes):
    return pltpu.CompilerParams(vmem_limit_bytes=mebibytes << 20)


def dot(left, right):
    return jnp.dot(left, right, preferred_element_type=F32)


def contract_rows(left, right):
    return lax.dot_general(left, right, (((0,), (0,)), ((), ())), preferred_element_type=F32)


def contract_cols(left, right):
    return lax.dot_general(left, right, (((1,), (1,)), ((), ())), preferred_element_type=F32)


def lane_tile(c):
    return slice(c * LANES, (c + 1) * LANES)


def split_kernel(count_ref, emit_ref, field_ref, kappa_ref, out_ref):
    blocks, _, rows, width = out_ref.shape
    cols = width - LANES
    lane = lax.broadcasted_iota(jnp.int32, (rows, LANES), 1)
    row = lax.broadcasted_iota(jnp.int32, (rows, LANES), 0)
    meta = jnp.zeros((rows, LANES), F32)
    for s in range(emit_ref.shape[1]):
        last = jnp.minimum(emit_ref[0, s], count_ref[0]) - 1
        meta = jnp.where((row == s) & (lane == STEPS), last.astype(F32), meta)
    none = jnp.zeros((rows, LANES), F32)
    for g in range(blocks):
        for part, ref in ((0, field_ref), (1, kappa_ref)):
            out_ref[g, part, :, :cols] = ref[0, :, g * cols : (g + 1) * cols]
            right = ref[0, :, (g + 1) * cols : (g + 1) * cols + LANES] if g < blocks - 1 else none
            left = ref[0, :, g * cols - LANES : g * cols] if g else none
            middle = meta if part == 0 else none
            out_ref[g, part, :, cols:] = jnp.where(
                lane < STEPS, right, jnp.where(lane >= LANES - STEPS, left, middle)
            )


def split_columns(initial, conductivity, step_count, emit_steps, blocks):
    _, rows, total = initial.shape
    width = total // blocks + LANES
    return pl.pallas_call(
        split_kernel,
        in_specs=[scalars, scalars, whole, whole],
        out_specs=whole,
        out_shape=jax.ShapeDtypeStruct((blocks, 2, rows, width), F32),
        compiler_params=params(16),
    )(step_count, emit_steps, initial, conductivity)


def solve_kernel(own_ref, top_ref, bottom_ref, out_ref, state, rate, bend, history):
    fields, _, rows, width = own_ref.shape
    tiles = width // LANES
    lane = lax.broadcasted_iota(jnp.int32, (8, LANES), 1)
    halo_lane = lax.broadcasted_iota(jnp.int32, (rows, LANES), 1)
    unused = (halo_lane >= STEPS) & (halo_lane < LANES - STEPS)
    first, last = lane == 0, lane == LANES - 1
    entries = fields * STEPS
    state[...] = jnp.zeros_like(state)

    def one_field(f, _):
        for j in range(tiles):
            for place, ref in enumerate((top_ref, own_ref, bottom_ref)):
                low = 8 + place * rows
                value = ref[f, 0, :, lane_tile(j)]
                if j == tiles - 1:
                    value = jnp.where(unused, 0.0, value)
                state[0, j, low : low + rows, :] = value
                kappa = ref[f, 1, :, lane_tile(j)] * step_rate
                rate[j, low : low + rows, :] = kappa
                bend[j, low : low + rows, :] = kappa * 0.25
        for part in range(STEPS // 8):

            def step(t, _):
                now = lax.rem(t, 2)
                later = 1 - now
                for tile in range(part, 3 * rows // 8 - part):
                    a = 8 + 8 * tile
                    middle = [state[now, j, a : a + 8, :] for j in range(tiles)]
                    west = [pltpu.roll(m, 1, 1) for m in middle]
                    east = [pltpu.roll(m, LANES - 1, 1) for m in middle]
                    for j in range(tiles):
                        beside = (state[now, j, a - 1 : a + 7, :] + state[now, j, a + 1 : a + 9, :]) + (
                            jnp.where(first, west[j - 1], west[j])
                            + jnp.where(last, east[(j + 1) % tiles], east[j])
                        )
                        gain = rate[j, a : a + 8, :] + bend[j, a : a + 8, :] * jnp.tanh(middle[j])
                        value = middle[j] + gain * (beside - 4.0 * middle[j])
                        state[later, j, a : a + 8, :] = value
                        if j < tiles - 1 and rows // 8 <= tile < 2 * rows // 8:
                            start = (8 * tile - rows) * entries + f * STEPS + t
                            history[j, pl.ds(start, 8, stride=entries), :] = value
                return 0

            lax.fori_loop(8 * part, 8 * part + 8, step, 0)
        return 0

    lax.fori_loop(0, fields, one_field, 0)
    out_ref[...] = history[...].astype(BF16)


def solve(own, top, bottom):
    fields, _, rows, width = own.shape
    tiles = width // LANES
    depth = 3 * rows + 16
    shape = (tiles - 1, rows * fields * STEPS, LANES)
    return pl.pallas_call(
        solve_kernel,
        in_specs=[whole, whole, whole],
        out_specs=whole,
        out_shape=jax.ShapeDtypeStruct(shape, BF16),
        scratch_shapes=[
            pltpu.VMEM((2, tiles, depth, LANES), F32),
            pltpu.VMEM((tiles, depth, LANES), F32),
            pltpu.VMEM((tiles, depth, LANES), F32),
            pltpu.VMEM(shape, F32),
        ],
        compiler_params=params(48),
    )(own, top, bottom)


def by_row_kernel(weight_ref, out_ref, wide):
    units, rows, cols = weight_ref.shape
    for c in range(cols // LANES):
        wide[c] = weight_ref[:, :, lane_tile(c)].astype(F32).reshape(units * rows, LANES)
    for r in range(rows):
        for c in range(cols // LANES):
            out_ref[r, :, lane_tile(c)] = wide[c, pl.ds(r, units, stride=rows), :].astype(BF16)


def by_row(weight, chunk=128):
    units, rows, cols = weight.shape
    return pl.pallas_call(
        by_row_kernel,
        grid=(units // chunk,),
        in_specs=[pl.BlockSpec((chunk, rows, cols), lambda i: (i, 0, 0))],
        out_specs=pl.BlockSpec((rows, chunk, cols), lambda i: (0, i, 0)),
        out_shape=jax.ShapeDtypeStruct((rows, units, cols), BF16),
        scratch_shapes=[pltpu.VMEM((cols // LANES, chunk * rows, LANES), F32)],
        compiler_params=params(32),
        cost_estimate=pl.CostEstimate(
            flops=0, bytes_accessed=4 * units * rows * cols, transcendentals=0
        ),
    )(weight)


def forward_kernel(inputs_ref, first_ref, second_ref, third_ref, a_ref, b_ref, c_ref, hid_ref):
    act = jnp.tanh(dot(inputs_ref[...], first_ref[...]))
    a_ref[...] = act
    act = jnp.tanh(dot(act.astype(BF16), second_ref[...]))
    b_ref[...] = act
    act = jnp.tanh(dot(act.astype(BF16), third_ref[...]))
    c_ref[...] = act
    hid_ref[...] = act.astype(BF16)


def forward(inputs, w_first, w_second, w_third):
    shape = (inputs.shape[0], w_first.shape[1])
    return pl.pallas_call(
        forward_kernel,
        in_specs=[whole] * 4,
        out_specs=[whole] * 4,
        out_shape=[jax.ShapeDtypeStruct(shape, F32)] * 3 + [jax.ShapeDtypeStruct(shape, BF16)],
        compiler_params=params(32),
    )(inputs, w_first, w_second, w_third)


def residual_kernel(scale, snaps, assign_ref, own_ref, hid_ref, weight_ref, history_ref, res_ref, back_ref, hot):
    rows, _, cols = weight_ref.shape
    fields = own_ref.shape[0]
    entries = fields * STEPS
    batch = hid_ref.shape[0]

    @pl.when(pl.program_id(0) == 0)
    def _():
        back_ref[...] = jnp.zeros_like(back_ref)
        lane = lax.broadcasted_iota(jnp.int32, (snaps, entries), 1)
        parts = []
        for f in range(fields):
            last = own_ref[f, 0, :snaps, STEPS : STEPS + 1].astype(jnp.int32)
            parts.append((lane == f * STEPS + last).astype(F32))
        steps = jnp.concatenate(parts, axis=0).astype(BF16)
        number = lax.broadcasted_iota(jnp.int32, (fields * snaps, batch), 0)
        chosen = (number == assign_ref[...]).astype(F32).astype(BF16)
        hot[...] = contract_rows(chosen, steps).astype(BF16)

    total = None
    for r in range(rows):
        predicted = dot(hid_ref[...], weight_ref[r])
        place = slice(r * entries, (r + 1) * entries)
        targets = [dot(hot[...], history_ref[c, place, :]) for c in range(cols // LANES)]
        residual = ((predicted - jnp.concatenate(targets, axis=1)) * scale).astype(BF16)
        res_ref[r] = residual
        back = contract_cols(residual, weight_ref[r])
        total = back if total is None else total + back
    back_ref[...] += total


def residual(assign, own, hidden, weight, history, snaps, chunk=4):
    rows, units, cols = weight.shape
    batch = hidden.shape[0]
    fields, _, _, width = own.shape
    entries = fields * STEPS
    scale = 1.0 / float(batch) ** 0.5
    return pl.pallas_call(
        functools.partial(residual_kernel, scale, snaps),
        grid=(rows // chunk,),
        in_specs=[
            pl.BlockSpec((1, batch), lambda i: (0, 0)),
            pl.BlockSpec((fields, 1, rows, LANES), lambda i: (0, 0, 0, width // LANES - 1)),
            pl.BlockSpec((batch, units), lambda i: (0, 0)),
            pl.BlockSpec((chunk, units, cols), lambda i: (i, 0, 0)),
            pl.BlockSpec((cols // LANES, chunk * entries, LANES), lambda i: (0, i, 0)),
        ],
        out_specs=[
            pl.BlockSpec((chunk, batch, cols), lambda i: (i, 0, 0)),
            pl.BlockSpec((batch, units), lambda i: (0, 0)),
        ],
        out_shape=[
            jax.ShapeDtypeStruct((rows, batch, cols), BF16),
            jax.ShapeDtypeStruct((batch, units), F32),
        ],
        scratch_shapes=[pltpu.VMEM((batch, entries), BF16)],
        compiler_params=params(48),
    )(assign.reshape(1, batch), own, hidden, weight, history)


def outer_kernel(hid_ref, res_ref, out_ref, wide):
    rows, _, cols = res_ref.shape
    units = out_ref.shape[0]
    for r in range(rows):
        grad = contract_rows(hid_ref[...], res_ref[r])
        for c in range(cols // LANES):
            wide[c, pl.ds(r, units, stride=rows), :] = grad[:, lane_tile(c)]
    for c in range(cols // LANES):
        out_ref[:, :, lane_tile(c)] = wide[c].reshape(units, rows, LANES).astype(BF16)


def outer(hidden, res, chunk=128):
    rows, batch, cols = res.shape
    units = hidden.shape[1]
    return pl.pallas_call(
        outer_kernel,
        grid=(units // chunk,),
        in_specs=[
            pl.BlockSpec((batch, chunk), lambda i: (0, i)),
            pl.BlockSpec((rows, batch, cols), lambda i: (0, 0, 0)),
        ],
        out_specs=pl.BlockSpec((chunk, rows, cols), lambda i: (i, 0, 0)),
        out_shape=jax.ShapeDtypeStruct((units, rows, cols), BF16),
        scratch_shapes=[pltpu.VMEM((cols // LANES, chunk * rows, LANES), F32)],
        compiler_params=params(48),
        cost_estimate=pl.CostEstimate(
            flops=2 * batch * units * rows * cols,
            bytes_accessed=4 * units * rows * cols,
            transcendentals=0,
        ),
    )(hidden, res)


def backward_kernel(inputs_ref, a_ref, b_ref, delta_ref, second_ref, third_ref, g1_ref, g2_ref, g3_ref):
    delta = delta_ref[...]
    act = b_ref[...]
    g3_ref[...] = contract_rows(act.astype(BF16), delta)
    delta = (contract_cols(delta, third_ref[...]) * (1.0 - act * act)).astype(BF16)
    act = a_ref[...]
    g2_ref[...] = contract_rows(act.astype(BF16), delta)
    delta = (contract_cols(delta, second_ref[...]) * (1.0 - act * act)).astype(BF16)
    g1_ref[...] = contract_rows(inputs_ref[...], delta)


def backward(inputs, act_a, act_b, delta, w_second, w_third):
    units = act_a.shape[1]
    return pl.pallas_call(
        backward_kernel,
        in_specs=[whole] * 6,
        out_specs=[whole] * 3,
        out_shape=[
            jax.ShapeDtypeStruct((inputs.shape[1], units), F32),
            jax.ShapeDtypeStruct((units, units), F32),
            jax.ShapeDtypeStruct((units, units), F32),
        ],
        compiler_params=params(32),
    )(inputs, act_a, act_b, delta, w_second, w_third)


def spread(block, count):
    copies = jnp.broadcast_to(block[None], (count,) + block.shape)
    got = lax.all_to_all(copies, ALL, split_axis=0, concat_axis=0, tiled=True)
    return got.reshape((-1,) + block.shape[1:])


def per_device(
    initial,
    conductivity,
    step_count,
    emit_steps,
    assign,
    sample_inputs,
    w_first,
    w_second,
    w_third,
    w_out,
):
    groups, strips = lax.axis_size("group"), lax.axis_size("strip")
    devices = groups * strips
    here = sample_inputs.shape[0]
    blocks = split_columns(initial, conductivity, step_count, emit_steps, groups)
    own = lax.all_to_all(blocks, "group", split_axis=0, concat_axis=0, tiled=True)
    down = [(i, i + 1) for i in range(strips - 1)]
    top = lax.ppermute(own, "strip", down)
    bottom = lax.ppermute(own, "strip", [(j, i) for i, j in down])
    inputs = spread(sample_inputs, devices)
    weight = by_row(w_out)
    act_a, act_b, act_c, hidden = forward(inputs, w_first, w_second, w_third)
    history = solve(own, top, bottom)
    res, partial = residual(assign, own, hidden, weight, history, emit_steps.shape[1])
    pieces = lax.all_to_all(
        partial.reshape(devices, here, -1), ALL, split_axis=0, concat_axis=0, tiled=True
    )
    grad_out = outer(hidden, res)
    mine = lax.axis_index(ALL) * here
    act_mine = lax.dynamic_slice_in_dim(act_c, mine, here, 0)
    delta_mine = (jnp.sum(pieces, axis=0) * (1.0 - act_mine * act_mine)).astype(BF16)
    delta = spread(delta_mine, devices)
    grads = backward(inputs, act_a, act_b, delta, w_second, w_third)
    return (*grads, grad_out)


def solution(mesh):
    placed = (
        P("group", "strip", None),
        P("group", "strip", None),
        P("group"),
        P("group", None),
        P(),
        P(("group", "strip"), None),
        P(),
        P(),
        P(),
        P(None, "strip", "group"),
    )
    return jax.shard_map(
        per_device,
        mesh=mesh,
        in_specs=placed,
        out_specs=(P(), P(), P(), P(None, "strip", "group")),
        check_vma=False,
    )
```

time: 476 us -> 132 us (0.28)
  waiting for transfers between devices: 242 us -> 10.4 us
  Pallas kernels: 0 us -> 68.9 us
  local copies, waits for them, and re-layouts: 63.8 us -> 17.9 us
  starting transfers between devices: 53.6 us -> 18.4 us
  blocking collectives: 43.4 us -> 12.1 us
  matrix products: 26.3 us -> 0 us
  loops' own time: 22 us -> 0 us
  between operations: 14.2 us -> 1.5 us
  other arithmetic: 8.46 us -> 1.74 us
    unnamed x3 -> x0, waiting for transfers between devices: 121 us -> none
    psum x1 -> x0, waiting for transfers between devices: 121 us -> none  [per_device(): lax.psum((partial_grads[0], partial_grads[1], partial_grads[2]), ('group'...]
    pallas_call x0 -> x7, Pallas kernels: none -> 68.9 us  [the longest x1 22.8 us: solve(): pl.pallas_call(solve_kernel, in_specs=[whole, whole, whole], out_specs=wh...]
    ppermute x18 -> x2, starting transfers between devices: 49.6 us -> 2.59 us  [the longest x1 1.3 us: per_device(): top = lax.ppermute(own, 'strip', down)]
    all_gather x1 -> x0, blocking collectives: 43.4 us -> none  [per_device(): lax.all_gather(hiddens[2], ('group', 'strip'), axis=0, tiled=True)]
    unnamed x23 -> x38, local copies, waits for them, and re-layouts: 42.3 us -> 14.1 us
    dot_general x10 -> x0, matrix products: 26.3 us -> none  [the longest x4 10.2 us: contract_rows(): lax.dot_general(left, right, (((0,), (0,)), ((), ())), preferred_element_...]
    another operation x1 -> x0, loops' own time: 22 us -> none  [per_device(): lax.fori_loop(0, STEPS // halo_width, block_steps, (field_now, start_hist...]
  transfers between devices with their start and end apart: 21 -> 5, of which waited for: 3 -> 1; matrix products, arithmetic and copies ran while one was open for 8% -> 1% of each run, Pallas kernels for 0% -> 26%
where the time goes in v1:
time: 132 us; the launch traced here: 131 us
  Pallas kernels  68.9 us (52%)
  starting transfers between devices  18.4 us (14%)
  local copies, waits for them, and re-layouts  17.9 us (14%)
  blocking collectives  12.1 us (9%)
  waiting for transfers between devices  10.4 us (8%)
  other arithmetic  1.74 us (1%)
  between operations  1.5 us (1%)
    pallas_call x1, Pallas kernels, solve(): pl.pallas_call(solve_kernel, in_specs=[whole, whole, whole], out_specs=wh...  22.8 us
    pallas_call x1, Pallas kernels, by_row(): pl.pallas_call(by_row_kernel, grid=(units // chunk,), in_specs=[pl.BlockS...  16.9 us
    pallas_call x1, Pallas kernels, outer(): pl.pallas_call(outer_kernel, grid=(units // chunk,), in_specs=[pl.BlockSp...  16 us
    unnamed x38, local copies, waits for them, and re-layouts  14.1 us
    all_to_all x1, blocking collectives, per_device(): lax.all_to_all(blocks, 'group', split_axis=0, concat_axis=0, tiled=True)  12.1 us
    all_to_all x1, waiting for transfers between devices, per_device(): lax.all_to_all(partial.reshape(devices, here, -1), ALL, split_axis=0, con...  10.4 us
    pallas_call x1, Pallas kernels, residual(): pl.pallas_call(functools.partial(residual_kernel, scale, snaps), grid=(ro...  10 us
    all_to_all x2, starting transfers between devices, spread(): got = lax.all_to_all(copies, ALL, split_axis=0, concat_axis=0, tiled=True)  9.85 us
  transfers between devices with their start and end apart: 5, of which 1 were waited for; matrix products, arithmetic and copies ran while one was open for 1% of the time, Pallas kernels for 26%

profile of v1, /device:TPU:0, one launch (start us, length us, event | category | flops | bytes accessed | tf_op | source)
XLA Modules:
  0.0 130.9 jit_solution(4318193582649308328)
XLA Ops:
  1.3 0.9 copy-done.13
  2.2 0.9 copy-done.14
  4.3 12.1 %all_to_all.20.own_ref = f32[4,2,32,384]{3,2,1,0:T(8,128)S(1)} all-to-all(f32[4,2,32,384]{3,2,1,0:T(8,128)S(1)} %shard_map.130), channel_id=1, replica_groups=mesh['group'=4,'strip'=8] {'group'}, dimensions={0} | all-to-all | bytes 786432 | tf_op jit(solution)/shard_map/all_to_all | solution.py:332
  16.4 1.3 collective-permute-start
  17.7 1.3 collective-permute-start.1
  19.0 1.3 broadcast_in_dim.4
  20.3 7.3 %all-to-all-start = ((bf16[32,4,128]{2,1,0:T(4,128)(2,1)}), bf16[32,4,128]{2,1,0:T(4,128)(2,1)S(1)}, u32[]{:S(2)}, u32[]{:S(2)}) async-start(bf16[32,4,128]{2,1,0:T(4,128)(2,1)} %broadcast_in_dim.4), calls=%async_computation | async-start | bytes 65536 | tf_op jit(solution)/shard_map/all_to_all | solution.py:312
  27.6 3.4 %copy-done.1 = bf16[512,32,256]{2,1,0:T(8,128)(2,1)S(1)} copy-done((bf16[512,32,256]{2,1,0:T(8,128)(2,1)S(1)}, bf16[512,32,256]{2,1,0:T(8,128)(2,1)}, u32[]{:S(2)}) %copy-start.1) | copy-done | bytes 8388632
  31.0 16.9 %shard_map.131.weight_ref = bf16[32,512,256]{2,1,0:T(8,128)(2,1)S(1)} custom-call(bf16[512,32,256]{2,1,0:T(8,128)(2,1)S(1)} %copy-done.1), custom_call_target="tpu_custom_call" | custom-call | bytes 16777216 | tf_op jit(solution)/shard_map/pallas_call | solution.py:156
  47.9 3.4 %copy-done = bf16[32,512,256]{2,1,0:T(8,128)(2,1)} copy-done((bf16[32,512,256]{2,1,0:T(8,128)(2,1)}, bf16[32,512,256]{2,1,0:T(8,128)(2,1)S(1)}, u32[]{:S(2)}) %copy-start) | copy-done | bytes 8388632
  52.5 0.7 copy-done.11
  53.2 22.8 %shard_map.132.history_ref = bf16[2,4096,128]{2,1,0:T(8,128)(2,1)S(1)} custom-call(f32[4,2,32,384]{3,2,1,0:T(8,128)S(1)} %all_to_all.20.own_ref, f32[4,2,32,384]{3,2,1,0:T(8,128)S(1)} %collective-permute-done.top_ref, f32[4,2,32,384]{3,2,1,0:T(8,128)S(1)} %collective-permute-done.1.bottom_ref), custom_call_target="tpu_custom_call" | custom-call | tf_op jit(solution)/shard_map/pallas_call | solution.py:130
  76.1 10.0 %shard_map.133 = (bf16[32,128,256]{2,1,0:T(8,128)(2,1)S(1)}, f32[128,512]{1,0:T(8,128)S(1)}) custom-call(s32[1,128]{1,0:T(1,128)S(1)} %bitcast.4, f32[4,2,32,384]{3,2,1,0:T(8,128)S(1)} %all_to_all.20.own_ref, bf16[128,512]{1,0:T(8,128)(2,1)S(1)} %get-tuple-element.15.hid_ref, bf16[32,512,256]{2,1,0:T(8,128)(2,1)} %copy-done, ...), custom_call_target="tpu_custom_call" | custom-call | tf_op jit(solution)/shard_map/pallas_call | solution.py:228
  86.8 1.7 %reshape.24 = f32[32,4,512]{2,1,0:T(4,128)} reshape(f32[128,512]{1,0:T(8,128)} %copy-done.8) | data formatting | bytes 524288 | tf_op jit(solution)/shard_map/reshape | solution.py:342
  88.5 6.0 %all-to-all-start.2 = ((f32[32,4,512]{2,1,0:T(4,128)}), f32[32,4,512]{2,1,0:T(4,128)}, u32[]{:S(2)}, u32[]{:S(2)}) async-start(f32[32,4,512]{2,1,0:T(4,128)} %reshape.24), calls=%async_computation.2 | async-start | bytes 524288 | tf_op jit(solution)/shard_map/all_to_all | solution.py:341
  94.5 10.4 %all-to-all-done.2 = f32[32,4,512]{2,1,0:T(4,128)} async-done(((f32[32,4,512]{2,1,0:T(4,128)}), f32[32,4,512]{2,1,0:T(4,128)}, u32[]{:S(2)}, u32[]{:S(2)}) %all-to-all-start.2) | async-done | bytes 262176 | tf_op jit(solution)/shard_map/all_to_all | solution.py:341
  104.8 1.0 reduce_sum.9
  105.9 0.7 multiply_convert_fusion
  107.3 2.6 %all-to-all-start.3 = ((bf16[32,4,512]{2,1,0:T(4,128)(2,1)}), bf16[32,4,512]{2,1,0:T(4,128)(2,1)S(1)}, u32[]{:S(2)}, u32[]{:S(2)}) async-start(bf16[32,4,512]{2,1,0:T(4,128)(2,1)} %broadcast_in_dim.5), calls=%async_computation.3 | async-start | bytes 262144 | tf_op jit(solution)/shard_map/all_to_all | solution.py:312
  109.9 0.9 copy-done.5
  110.8 16.0 %shard_map.135 = bf16[512,32,256]{2,1,0:T(8,128)(2,1)} custom-call(bf16[128,512]{1,0:T(8,128)(2,1)S(1)} %copy-done.5, bf16[32,128,256]{2,1,0:T(8,128)(2,1)S(1)} %get-tuple-element.21.res_ref), custom_call_target="tpu_custom_call" | custom-call | flops 1073741824 | bytes 16777216 | tf_op jit(solution)/shard_map/pallas_call | solution.py:265
  126.8 0.9 copy-done.10
  127.8 0.9 copy-done.12
  128.7 2.2 %shard_map.134 = (f32[128,512]{1,0:T(8,128)}, f32[512,512]{1,0:T(8,128)}, f32[512,512]{1,0:T(8,128)}) custom-call(bf16[128,128]{1,0:T(8,128)(2,1)S(1)} %bitcast.3, f32[128,512]{1,0:T(8,128)S(1)} %copy-done.10, f32[128,512]{1,0:T(8,128)S(1)} %copy-done.12, bf16[128,512]{1,0:T(8,128)(2,1)S(1)} %reshape.25.delta_ref, bf16[512,512]{1,0:T(8,128)(2,1)S(1)} %copy-done.2, ...), custom_call_target="tpu_custom_call" | custom-call | tf_op jit(solution)/shard_map/pallas_call | solution.py:297
  (38 shorter events, 3.9 us)
Async XLA Ops:
  1.3 0.9 copy-start.13
  2.2 0.9 copy-start.14
  3.1 0.7 copy-start.16
  16.4 36.8 %collective-permute-start = (f32[4,2,32,384]{3,2,1,0:T(8,128)S(1)}, f32[4,2,32,384]{3,2,1,0:T(8,128)S(1)}, u32[]{:S(2)}, u32[]{:S(2)}) collective-permute-start(f32[4,2,32,384]{3,2,1,0:T(8,128)S(1)} %all_to_all.20.own_ref), channel_id=1, source_target_pairs={{0,1},{1,2},{2,3},{3,4},{4,5},{5,6},{6,7},{8,9},{9,10},{10,11},{11... | collective-permute-start | bytes 1179656 | tf_op jit(solution)/shard_map/ppermute | solution.py:334
  17.7 35.5 %collective-permute-start.1 = (f32[4,2,32,384]{3,2,1,0:T(8,128)S(1)}, f32[4,2,32,384]{3,2,1,0:T(8,128)S(1)}, u32[]{:S(2)}, u32[]{:S(2)}) collective-permute-start(f32[4,2,32,384]{3,2,1,0:T(8,128)S(1)} %all_to_all.20.own_ref), channel_id=1, source_target_pairs={{1,0},{2,1},{3,2},{4,3},{5,4},{6,5},{7,6},{9,8},{10,9},{11,10},{12... | collective-permute-start | bytes 1179656 | tf_op jit(solution)/shard_map/ppermute | solution.py:335
  20.3 31.0 %all-to-all-start = ((bf16[32,4,128]{2,1,0:T(4,128)(2,1)}), bf16[32,4,128]{2,1,0:T(4,128)(2,1)S(1)}, u32[]{:S(2)}, u32[]{:S(2)}) async-start(bf16[32,4,128]{2,1,0:T(4,128)(2,1)} %broadcast_in_dim.4), calls=%async_computation | async-start | bytes 65536 | tf_op jit(solution)/shard_map/all_to_all | solution.py:312
  27.6 3.4 %copy-start.1 = (bf16[512,32,256]{2,1,0:T(8,128)(2,1)S(1)}, bf16[512,32,256]{2,1,0:T(8,128)(2,1)}, u32[]{:S(2)}) copy-start(bf16[512,32,256]{2,1,0:T(8,128)(2,1)} %weight_ref.1) | copy-start | bytes 25165828
  31.0 20.3 %copy-start.2 = (bf16[512,512]{1,0:T(8,128)(2,1)S(1)}, bf16[512,512]{1,0:T(8,128)(2,1)}, u32[]{:S(2)}) copy-start(bf16[512,512]{1,0:T(8,128)(2,1)} %second_ref.3) | copy-start | bytes 1572868
  31.0 20.3 %copy-start.3 = (bf16[512,512]{1,0:T(8,128)(2,1)S(1)}, bf16[512,512]{1,0:T(8,128)(2,1)}, u32[]{:S(2)}) copy-start(bf16[512,512]{1,0:T(8,128)(2,1)} %third_ref.3) | copy-start | bytes 1572868
  31.0 20.3 %copy-start.15 = (bf16[128,512]{1,0:T(8,128)(2,1)S(1)}, bf16[128,512]{1,0:T(8,128)(2,1)}, u32[]{:S(2)}) copy-start(bf16[128,512]{1,0:T(8,128)(2,1)} %first_ref.1) | copy-start | bytes 393220
  31.0 45.0 %copy-start.17 = (s32[128]{0:T(128)S(1)}, s32[128]{0:T(128)}, u32[]{:S(2)}) copy-start(s32[128]{0:T(128)} %param.14) | copy-start | bytes 1540
  47.9 3.4 %copy-start = (bf16[32,512,256]{2,1,0:T(8,128)(2,1)}, bf16[32,512,256]{2,1,0:T(8,128)(2,1)S(1)}, u32[]{:S(2)}) copy-start(bf16[32,512,256]{2,1,0:T(8,128)(2,1)S(1)} %shard_map.131.weight_ref) | copy-start | bytes 25165828
  51.3 24.8 %copy-start.6 = (bf16[32,4,128]{2,1,0:T(4,128)(2,1)}, bf16[32,4,128]{2,1,0:T(4,128)(2,1)S(1)}, u32[]{:S(2)}) copy-start(bf16[32,4,128]{2,1,0:T(4,128)(2,1)S(1)} %all-to-all-done) | copy-start | bytes 98308
  51.8 0.7 copy-start.9
  52.5 0.7 copy-start.11
  53.2 22.8 %copy-start.18 = (f32[128,512]{1,0:T(8,128)}, f32[128,512]{1,0:T(8,128)S(1)}, u32[]{:S(2)}) copy-start(f32[128,512]{1,0:T(8,128)S(1)} %get-tuple-element.17) | copy-start | bytes 786436
  53.2 32.8 %copy-start.4 = (bf16[128,512]{1,0:T(8,128)(2,1)}, bf16[128,512]{1,0:T(8,128)(2,1)S(1)}, u32[]{:S(2)}) copy-start(bf16[128,512]{1,0:T(8,128)(2,1)S(1)} %get-tuple-element.15.hid_ref) | copy-start | bytes 393220
  86.1 0.7 copy-start.8
  86.8 40.0 %copy-start.7 = (bf16[32,4,128]{2,1,0:T(4,128)(2,1)S(1)}, bf16[32,4,128]{2,1,0:T(4,128)(2,1)}, u32[]{:S(2)}) copy-start(bf16[32,4,128]{2,1,0:T(4,128)(2,1)} %copy-done.6) | copy-start | bytes 98308
  88.5 16.3 %all-to-all-start.2 = ((f32[32,4,512]{2,1,0:T(4,128)}), f32[32,4,512]{2,1,0:T(4,128)}, u32[]{:S(2)}, u32[]{:S(2)}) async-start(f32[32,4,512]{2,1,0:T(4,128)} %reshape.24), calls=%async_computation.2 | async-start | bytes 524288 | tf_op jit(solution)/shard_map/all_to_all | solution.py:341
  107.3 19.5 %all-to-all-start.3 = ((bf16[32,4,512]{2,1,0:T(4,128)(2,1)}), bf16[32,4,512]{2,1,0:T(4,128)(2,1)S(1)}, u32[]{:S(2)}, u32[]{:S(2)}) async-start(bf16[32,4,512]{2,1,0:T(4,128)(2,1)} %broadcast_in_dim.5), calls=%async_computation.3 | async-start | bytes 262144 | tf_op jit(solution)/shard_map/all_to_all | solution.py:312
  109.9 0.9 copy-start.5
  126.8 1.0 copy-start.10
  127.8 0.9 copy-start.12

commit v2 on v1

v2 whole, which is shorter than its diff:
```python
import functools

import jax
import jax.numpy as jnp
from jax import lax
from jax.experimental import pallas as pl
from jax.experimental.pallas import tpu as pltpu
from jax.sharding import PartitionSpec as P

STEPS = 32
LANES = 128
META = 120
step_rate = 0.125

BF16 = jnp.bfloat16
F32 = jnp.float32
ALL = ("group", "strip")
whole = pl.BlockSpec(memory_space=pltpu.VMEM)
scalars = pl.BlockSpec(memory_space=pltpu.SMEM)


def params(mebibytes):
    return pltpu.CompilerParams(vmem_limit_bytes=mebibytes << 20)


def dot(left, right):
    return jnp.dot(left, right, preferred_element_type=F32)


def contract_rows(left, right):
    return lax.dot_general(left, right, (((0,), (0,)), ((), ())), preferred_element_type=F32)


def contract_cols(left, right):
    return lax.dot_general(left, right, (((1,), (1,)), ((), ())), preferred_element_type=F32)


def lane_tile(c):
    return slice(c * LANES, (c + 1) * LANES)


def tiles_for(cols):
    return -(-(cols + 2 * STEPS) // LANES)


def split_kernel(count_ref, emit_ref, field_ref, kappa_ref, inputs_ref, out_ref, seed_ref):
    blocks, _, rows, width = out_ref.shape
    tiles = width // LANES
    total = field_ref.shape[2]
    cols = total // blocks
    span = cols + 2 * LANES
    source = lax.broadcasted_iota(jnp.int32, (span, width), 0) - (LANES - STEPS)
    place = lax.broadcasted_iota(jnp.int32, (span, width), 1)
    wanted = tiles * (place % LANES) + place // LANES
    deal = ((source == wanted) & (wanted < cols + 2 * STEPS)).astype(F32).astype(BF16)
    none = jnp.zeros((2 * rows, LANES), F32)
    both = jnp.concatenate([field_ref[0], kappa_ref[0]], axis=0)
    both = jnp.concatenate([none, both, none], axis=1)
    high = both.astype(BF16)
    rest = both - high.astype(F32)
    middle = rest.astype(BF16)
    low = (rest - middle.astype(F32)).astype(BF16)
    lane = lax.broadcasted_iota(jnp.int32, (rows, LANES), 1)
    row = lax.broadcasted_iota(jnp.int32, (rows, LANES), 0)
    meta = jnp.zeros((rows, LANES), F32)
    for s in range(emit_ref.shape[1]):
        last = jnp.minimum(emit_ref[0, s], count_ref[0]) - 1
        meta = jnp.where(row == s, last.astype(F32), meta)
    for g in range(blocks):
        window = slice(g * cols, g * cols + span)
        dealt = dot(high[:, window], deal) + dot(middle[:, window], deal) + dot(low[:, window], deal)
        out_ref[g, 0] = dealt[:rows]
        out_ref[g, 1] = dealt[rows:]
        out_ref[g, 0, :, :LANES] = jnp.where(lane == META, meta, dealt[:rows, :LANES])
    here = inputs_ref.shape[0]
    devices, deep, features = seed_ref.shape
    seed = inputs_ref[...].astype(F32)
    if deep > here:
        seed = jnp.concatenate([seed, jnp.zeros((deep - here, features), F32)], axis=0)
    for d in range(devices):
        seed_ref[d] = seed


def split_columns(initial, conductivity, step_count, emit_steps, inputs, blocks, devices):
    _, rows, total = initial.shape
    width = tiles_for(total // blocks) * LANES
    here, features = inputs.shape
    return pl.pallas_call(
        split_kernel,
        in_specs=[scalars, scalars, whole, whole, whole],
        out_specs=[whole, whole],
        out_shape=[
            jax.ShapeDtypeStruct((blocks, 2, rows, width), F32),
            jax.ShapeDtypeStruct((devices, -(-here // 8) * 8, features), F32),
        ],
        compiler_params=params(60),
    )(step_count, emit_steps, initial, conductivity, inputs)


def advance(state, rate, bend, history, pitch, part, fields, now, t):
    _, _, tiles, depth, _ = state.shape
    rows = (depth - 16) // 3
    later = 1 - now
    for tile in range(part, 3 * rows // 8 - part):
        a = 8 + 8 * tile
        for f in fields:
            middle = [state[f, now, j, a : a + 8, :] for j in range(tiles)]
            west = [pltpu.roll(middle[-1], 1, 1)] + middle[:-1]
            east = middle[1:] + [pltpu.roll(middle[0], LANES - 1, 1)]
            for j in range(tiles):
                north = state[f, now, j, a - 1 : a + 7, :]
                south = state[f, now, j, a + 1 : a + 9, :]
                beside = (north + south) + (west[j] + east[j])
                gain = rate[f, j, a : a + 8, :] + bend[f, j, a : a + 8, :] * jnp.tanh(middle[j])
                value = middle[j] + gain * (beside - 4.0 * middle[j])
                state[f, later, j, a : a + 8, :] = value
                if rows <= 8 * tile < 2 * rows:
                    start = (8 * tile - rows) * pitch + f * STEPS + t
                    history[j, pl.ds(start, 8, stride=pitch), :] = value


def residual_kernel(
    scale, snaps, assign_ref, own_ref, top_ref, bottom_ref, predicted_ref, weight_ref,
    res_ref, back_ref, state, rate, bend, history, picked, weight, total, arrived,
):
    fields, _, rows, width = own_ref.shape
    _, batch, cols = predicted_ref.shape
    tiles = width // LANES
    entries = fields * STEPS
    pitch = entries + 1
    copy = pltpu.make_async_copy(weight_ref, weight, arrived)
    copy.start()

    state[...] = jnp.zeros_like(state)
    for f in range(fields):
        for j in range(tiles):
            for place, ref in enumerate((top_ref, own_ref, bottom_ref)):
                low = 8 + place * rows
                state[f, 0, j, low : low + rows, :] = ref[f, 0, :, lane_tile(j)]
                kappa = ref[f, 1, :, lane_tile(j)] * step_rate
                rate[f, j, low : low + rows, :] = kappa
                bend[f, j, low : low + rows, :] = kappa * 0.25
    together = 2 if fields % 2 == 0 else 1

    def some_fields(g, _):
        which = [g * together + i for i in range(together)]
        for part in range(STEPS // 8):

            def two_steps(pair, _):
                for now in range(2):
                    advance(state, rate, bend, history, pitch, part, which, now, 2 * pair + now)
                return 0

            lax.fori_loop(4 * part, 4 * part + 4, two_steps, 0)
        return 0

    lax.fori_loop(0, fields // together, some_fields, 0)

    lane = lax.broadcasted_iota(jnp.int32, (snaps, entries), 1)
    steps = []
    for f in range(fields):
        last = own_ref[f, 0, :snaps, META : META + 1].astype(jnp.int32)
        steps.append((lane == f * STEPS + last).astype(F32))
    steps = jnp.concatenate(steps, axis=0).astype(BF16)
    number = lax.broadcasted_iota(jnp.int32, (fields * snaps, batch), 0)
    chosen = (number == assign_ref[...]).astype(F32).astype(BF16)
    hot = contract_rows(chosen, steps).astype(BF16)
    place = lax.broadcasted_iota(jnp.int32, (width, cols), 0)
    column = lax.broadcasted_iota(jnp.int32, (width, cols), 1) + STEPS
    gather = (tiles * (place % LANES) + place // LANES == column).astype(F32).astype(BF16)

    for r in range(rows):
        for j in range(tiles):
            states = history[j, r * pitch : r * pitch + entries, :].astype(BF16)
            picked[r, :, lane_tile(j)] = dot(hot, states).astype(BF16)
    copy.wait()
    total[...] = jnp.zeros_like(total)

    def some_rows(i, _):
        back = None
        for k in range(chunk):
            r = i * chunk + k
            targets = dot(picked[r], gather)
            residual = ((predicted_ref[r] - targets) * scale).astype(BF16)
            res_ref[r] = residual
            part = contract_cols(residual, weight[r])
            back = part if back is None else back + part
        total[...] += back
        return 0

    chunk = 8
    lax.fori_loop(0, rows // chunk, some_rows, 0)
    devices, _, folded = back_ref.shape
    here = batch // devices
    for d in range(devices):
        for k in range(total.shape[1] // folded):
            back_ref[d, k * here : (k + 1) * here, :] = total[
                d * here : (d + 1) * here, k * folded : (k + 1) * folded
            ]


def residual(assign, own, top, bottom, predicted, weight, snaps, devices, fold):
    rows, units, cols = weight.shape
    batch = predicted.shape[1]
    fields, _, _, width = own.shape
    tiles = width // LANES
    depth = 3 * rows + 16
    entries = fields * STEPS
    here = batch // devices
    scale = 1.0 / float(batch) ** 0.5
    return pl.pallas_call(
        functools.partial(residual_kernel, scale, snaps),
        in_specs=[whole] * 5 + [pl.BlockSpec(memory_space=pl.ANY)],
        out_specs=[whole, whole],
        out_shape=[
            jax.ShapeDtypeStruct((rows, batch, cols), BF16),
            jax.ShapeDtypeStruct((devices, here * fold, units // fold), F32),
        ],
        scratch_shapes=[
            pltpu.VMEM((fields, 2, tiles, depth, LANES), F32),
            pltpu.VMEM((fields, tiles, depth, LANES), F32),
            pltpu.VMEM((fields, tiles, depth, LANES), F32),
            pltpu.VMEM((tiles, rows * (entries + 1), LANES), F32),
            pltpu.VMEM((rows, batch, width), BF16),
            pltpu.VMEM((rows, units, cols), BF16),
            pltpu.VMEM((batch, units), F32),
            pltpu.SemaphoreType.DMA,
        ],
        compiler_params=params(60),
    )(assign.reshape(1, batch), own, top, bottom, predicted, weight)


def by_row_kernel(weight_ref, out_ref):
    units, rows, cols = weight_ref.shape
    for c in range(cols // LANES):
        for u in range(0, units, 16):
            for r in range(0, rows, 16):
                block = weight_ref[u : u + 16, r : r + 16, lane_tile(c)]
                out_ref[r : r + 16, u : u + 16, lane_tile(c)] = jnp.swapaxes(block, 0, 1)


def by_row(weight, chunk=128):
    units, rows, cols = weight.shape
    return pl.pallas_call(
        by_row_kernel,
        grid=(units // chunk,),
        in_specs=[pl.BlockSpec((chunk, rows, cols), lambda i: (i, 0, 0))],
        out_specs=pl.BlockSpec((rows, chunk, cols), lambda i: (0, i, 0)),
        out_shape=jax.ShapeDtypeStruct((rows, units, cols), BF16),
        compiler_params=params(60),
        cost_estimate=pl.CostEstimate(
            flops=0, bytes_accessed=4 * units * rows * cols, transcendentals=0
        ),
    )(weight)


def fold_rows(value, out_ref, scratch):
    devices, deep, folded = out_ref.shape
    batch, units = value.shape
    here = batch // devices
    scratch[...] = value
    for d in range(devices):
        for k in range(units // folded):
            out_ref[d, k * here : (k + 1) * here, :] = scratch[
                d * here : (d + 1) * here, k * folded : (k + 1) * folded
            ]


def forward_kernel(
    seed_ref, first_ref, second_ref, third_ref, in_ref, a_ref, b_ref, hid_ref, gate_ref, inputs, scratch
):
    devices = seed_ref.shape[0]
    here = in_ref.shape[0] // devices
    for d in range(devices):
        inputs[d * here : (d + 1) * here, :] = seed_ref[d, :here, :]
    in_ref[...] = inputs[...].astype(BF16)
    act = jnp.tanh(dot(in_ref[...], first_ref[...]))
    a_ref[...] = act
    act = jnp.tanh(dot(act.astype(BF16), second_ref[...]))
    b_ref[...] = act
    act = jnp.tanh(dot(act.astype(BF16), third_ref[...]))
    hid_ref[...] = act.astype(BF16)
    fold_rows(1.0 - act * act, gate_ref, scratch)


def forward(seeds, w_first, w_second, w_third, here, fold):
    devices = seeds.shape[0]
    features, units = w_first.shape
    batch = devices * here
    shape = (batch, units)
    return pl.pallas_call(
        forward_kernel,
        in_specs=[whole] * 4,
        out_specs=[whole] * 5,
        out_shape=[
            jax.ShapeDtypeStruct((batch, features), BF16),
            jax.ShapeDtypeStruct(shape, F32),
            jax.ShapeDtypeStruct(shape, F32),
            jax.ShapeDtypeStruct(shape, BF16),
            jax.ShapeDtypeStruct((devices, here * fold, units // fold), F32),
        ],
        scratch_shapes=[pltpu.VMEM((batch, features), F32), pltpu.VMEM(shape, F32)],
        compiler_params=params(60),
    )(seeds, w_first, w_second, w_third)


def predict_kernel(hid_ref, weight_ref, out_ref):
    for r in range(weight_ref.shape[0]):
        out_ref[r] = dot(hid_ref[...], weight_ref[r])


def predict(hidden, weight, chunk=8):
    rows, units, cols = weight.shape
    batch = hidden.shape[0]
    return pl.pallas_call(
        predict_kernel,
        grid=(rows // chunk,),
        in_specs=[
            pl.BlockSpec((batch, units), lambda i: (0, 0)),
            pl.BlockSpec((chunk, units, cols), lambda i: (i, 0, 0)),
        ],
        out_specs=pl.BlockSpec((chunk, batch, cols), lambda i: (i, 0, 0)),
        out_shape=jax.ShapeDtypeStruct((rows, batch, cols), F32),
        compiler_params=params(60),
    )(hidden, weight)


def outer_kernel(hid_ref, res_ref, out_ref, grads):
    rows, _, cols = res_ref.shape
    units = out_ref.shape[0]
    for r in range(rows):
        grads[r] = contract_rows(hid_ref[...], res_ref[r]).astype(BF16)
    for c in range(cols // LANES):
        for u in range(0, units, 16):
            for r in range(0, rows, 16):
                block = grads[r : r + 16, u : u + 16, lane_tile(c)]
                out_ref[u : u + 16, r : r + 16, lane_tile(c)] = jnp.swapaxes(block, 0, 1)


def outer(hidden, res, chunk=128):
    rows, batch, cols = res.shape
    units = hidden.shape[1]
    return pl.pallas_call(
        outer_kernel,
        grid=(units // chunk,),
        in_specs=[
            pl.BlockSpec((batch, chunk), lambda i: (0, i)),
            pl.BlockSpec((rows, batch, cols), lambda i: (0, 0, 0)),
        ],
        out_specs=pl.BlockSpec((chunk, rows, cols), lambda i: (i, 0, 0)),
        out_shape=jax.ShapeDtypeStruct((units, rows, cols), BF16),
        scratch_shapes=[pltpu.VMEM((rows, chunk, cols), BF16)],
        compiler_params=params(60),
        cost_estimate=pl.CostEstimate(
            flops=2 * batch * units * rows * cols,
            bytes_accessed=4 * units * rows * cols,
            transcendentals=0,
        ),
    )(hidden, res)


def delta_kernel(here_ref, pieces_ref, gate_ref, out_ref):
    devices = pieces_ref.shape[0]
    back = pieces_ref[0]
    for d in range(1, devices):
        back = back + pieces_ref[d]
    delta = (back * gate_ref[here_ref[0]]).astype(BF16)
    for d in range(devices):
        out_ref[d] = delta


def delta_spread(place, pieces, gate):
    return pl.pallas_call(
        delta_kernel,
        in_specs=[scalars, whole, whole],
        out_specs=whole,
        out_shape=jax.ShapeDtypeStruct(pieces.shape, BF16),
        compiler_params=params(60),
    )(place.reshape(1), pieces, gate)


def backward_kernel(
    inputs_ref, a_ref, b_ref, delta_ref, second_ref, third_ref, g1_ref, g2_ref, g3_ref, folded, unfolded
):
    devices, deep, width = delta_ref.shape
    batch, units = a_ref.shape
    here = batch // devices
    folded[...] = delta_ref[...].astype(F32)
    for d in range(devices):
        for k in range(units // width):
            unfolded[d * here : (d + 1) * here, k * width : (k + 1) * width] = folded[
                d, k * here : (k + 1) * here, :
            ]
    delta = unfolded[...].astype(BF16)
    act = b_ref[...]
    g3_ref[...] = contract_rows(act.astype(BF16), delta)
    delta = (contract_cols(delta, third_ref[...]) * (1.0 - act * act)).astype(BF16)
    act = a_ref[...]
    g2_ref[...] = contract_rows(act.astype(BF16), delta)
    delta = (contract_cols(delta, second_ref[...]) * (1.0 - act * act)).astype(BF16)
    g1_ref[...] = contract_rows(inputs_ref[...], delta)


def backward(inputs, act_a, act_b, delta, w_second, w_third):
    batch, units = act_a.shape
    return pl.pallas_call(
        backward_kernel,
        in_specs=[whole] * 6,
        out_specs=[whole] * 3,
        out_shape=[
            jax.ShapeDtypeStruct((inputs.shape[1], units), F32),
            jax.ShapeDtypeStruct((units, units), F32),
            jax.ShapeDtypeStruct((units, units), F32),
        ],
        scratch_shapes=[pltpu.VMEM(delta.shape, F32), pltpu.VMEM((batch, units), F32)],
        compiler_params=params(60),
    )(inputs, act_a, act_b, delta, w_second, w_third)


def swap(value, axes):
    return lax.all_to_all(value, axes, split_axis=0, concat_axis=0, tiled=True)


def per_device(
    initial,
    conductivity,
    step_count,
    emit_steps,
    assign,
    sample_inputs,
    w_first,
    w_second,
    w_third,
    w_out,
):
    groups, strips = lax.axis_size("group"), lax.axis_size("strip")
    devices = groups * strips
    here = sample_inputs.shape[0]
    fold = max(1, 8 // here)
    blocks, seeds = split_columns(
        initial, conductivity, step_count, emit_steps, sample_inputs, groups, devices
    )
    blocks, seeds, w_out = lax.optimization_barrier((blocks, seeds, w_out))
    own = swap(blocks, "group")
    seeds = swap(seeds, ALL)
    weight = by_row(w_out)
    own, weight = lax.optimization_barrier((own, weight))
    down = [(i, i + 1) for i in range(strips - 1)]
    top = lax.ppermute(own, "strip", down)
    bottom = lax.ppermute(own, "strip", [(j, i) for i, j in down])
    inputs, act_a, act_b, hidden, gate = forward(seeds, w_first, w_second, w_third, here, fold)
    predicted = predict(hidden, weight)
    res, partial = residual(
        assign, own, top, bottom, predicted, weight, emit_steps.shape[1], devices, fold
    )
    pieces = swap(partial, ALL)
    grad_out = outer(hidden, res)
    pieces, grad_out = lax.optimization_barrier((pieces, grad_out))
    delta = swap(delta_spread(lax.axis_index(ALL), pieces, gate), ALL)
    grads = backward(inputs, act_a, act_b, delta, w_second, w_third)
    return (*grads, grad_out)


def solution(mesh):
    placed = (
        P("group", "strip", None),
        P("group", "strip", None),
        P("group"),
        P("group", None),
        P(),
        P(("group", "strip"), None),
        P(),
        P(),
        P(),
        P(None, "strip", "group"),
    )
    return jax.shard_map(
        per_device,
        mesh=mesh,
        in_specs=placed,
        out_specs=(P(), P(), P(), P(None, "strip", "group")),
        check_vma=False,
    )
```

time: 132 us -> 97.4 us (0.74)
  Pallas kernels: 68.9 us -> 52 us
  blocking collectives: 12.1 us -> 29 us
  local copies, waits for them, and re-layouts: 17.9 us -> 1.58 us
  waiting for transfers between devices: 10.4 us -> 2.33 us
  starting transfers between devices: 18.4 us -> 10.5 us
  other arithmetic: 1.74 us -> 0 us
    all_to_all x1 -> x2, blocking collectives: 12.1 us -> 29 us  [swap(): return lax.all_to_all(value, axes, split_axis=0, concat_axis=0, tiled=True)]
    unnamed x38 -> x10, local copies, waits for them, and re-layouts: 14.1 us -> 1.58 us
    pallas_call x1, Pallas kernels: 16.9 us -> 8.02 us  [by_row(): pl.pallas_call(by_row_kernel, grid=(units // chunk,), in_specs=[pl.BlockS...]
    all_to_all x3 -> x2, starting transfers between devices: 15.8 us -> 7.76 us  [swap(): return lax.all_to_all(value, axes, split_axis=0, concat_axis=0, tiled=True)]
    all_to_all x3 -> x2, waiting for transfers between devices: 10.4 us -> 2.33 us  [swap(): return lax.all_to_all(value, axes, split_axis=0, concat_axis=0, tiled=True)]
    pallas_call x1, Pallas kernels: 16 us -> 8.05 us  [outer(): pl.pallas_call(outer_kernel, grid=(units // chunk,), in_specs=[pl.BlockSp...]
    pallas_call x3 -> x4, Pallas kernels: 33.4 us -> 29.7 us  [the longest x1 18.8 us: residual(): pl.pallas_call(functools.partial(residual_kernel, scale, snaps), in_specs...]
    pallas_call x1, Pallas kernels: 0.52 us -> 2.67 us  [forward(): pl.pallas_call(forward_kernel, in_specs=[whole] * 4, out_specs=[whole] *...]
  transfers between devices with their start and end apart: 5 -> 4, of which waited for: 1 -> 1; matrix products, arithmetic and copies ran while one was open for 1% -> 0% of each run, Pallas kernels for 26% -> 26%
where the time goes in v2:
time: 97.4 us; the launch traced here: 96.8 us
  Pallas kernels  52 us (53%)
  blocking collectives  29 us (30%)
  starting transfers between devices  10.5 us (11%)
  waiting for transfers between devices  2.33 us (2%)
  local copies, waits for them, and re-layouts  1.58 us (2%)
  between operations  1.35 us (1%)
    all_to_all x2, blocking collectives, swap(): return lax.all_to_all(value, axes, split_axis=0, concat_axis=0, tiled=True)  29 us
    pallas_call x1, Pallas kernels, residual(): pl.pallas_call(functools.partial(residual_kernel, scale, snaps), in_specs...  18.8 us
    pallas_call x1, Pallas kernels, outer(): pl.pallas_call(outer_kernel, grid=(units // chunk,), in_specs=[pl.BlockSp...  8.05 us
    pallas_call x1, Pallas kernels, by_row(): pl.pallas_call(by_row_kernel, grid=(units // chunk,), in_specs=[pl.BlockS...  8.02 us
    all_to_all x2, starting transfers between devices, swap(): return lax.all_to_all(value, axes, split_axis=0, concat_axis=0, tiled=True)  7.76 us
    pallas_call x1, Pallas kernels, predict(): pl.pallas_call(predict_kernel, grid=(rows // chunk,), in_specs=[pl.BlockS...  6.5 us
    pallas_call x1, Pallas kernels, backward(): pl.pallas_call(backward_kernel, in_specs=[whole] * 6, out_specs=[whole] *...  3.61 us
    pallas_call x1, Pallas kernels, forward(): pl.pallas_call(forward_kernel, in_specs=[whole] * 4, out_specs=[whole] *...  2.67 us
  transfers between devices with their start and end apart: 4, of which 1 were waited for; matrix products, arithmetic and copies ran while one was open for 0% of the time, Pallas kernels for 26%

profile of v2, /device:TPU:0, one launch (start us, length us, event | category | flops | bytes accessed | tf_op | source)
XLA Modules:
  0.0 96.8 jit_solution(11397071636903710836)
XLA Ops:
  1.3 2.6 %shard_map.129 = (f32[4,2,32,384]{3,2,1,0:T(8,128)}, f32[32,8,128]{2,1,0:T(8,128)}) custom-call(s32[1]{0:T(128)S(6)} %copy.14.count_ref, s32[1,16]{1,0:T(1,128)} %emit_ref.1, f32[1,32,1024]{2,1,0:T(8,128)} %field_ref.1, f32[1,32,1024]{2,1,0:T(8,128)} %kappa_ref.1, bf16[4,128]{1,0:T(4,128)(2,1)} %inputs_ref.1), custom_call_target="tpu_custom_call" | custom-call | tf_op jit(solution)/shard_map/pallas_call | solution.py:88
  3.9 5.2 %all-to-all-start.1 = ((f32[4,2,32,384]{3,2,1,0:T(8,128)}), f32[4,2,32,384]{3,2,1,0:T(8,128)S(1)}, u32[]{:S(2)}, u32[]{:S(2)}) async-start(f32[4,2,32,384]{3,2,1,0:T(8,128)} %get-tuple-element.29), calls=%async_computation.1 | async-start | bytes 786432 | tf_op jit(solution)/shard_map/all_to_all | solution.py:421
  9.1 8.0 %shard_map.131.weight_ref = bf16[32,512,256]{2,1,0:T(8,128)(2,1)} custom-call(bf16[512,32,256]{2,1,0:T(8,128)(2,1)} %weight_ref), custom_call_target="tpu_custom_call" | custom-call | bytes 16777216 | tf_op jit(solution)/shard_map/pallas_call | solution.py:244
  17.1 0.0 all-to-all-done.1.own_ref
  17.1 1.5 %collective-permute-start = (f32[4,2,32,384]{3,2,1,0:T(8,128)S(1)}, f32[4,2,32,384]{3,2,1,0:T(8,128)S(1)}, u32[]{:S(2)}, u32[]{:S(2)}) collective-permute-start(f32[4,2,32,384]{3,2,1,0:T(8,128)S(1)} %all-to-all-done.1.own_ref), channel_id=1, source_target_pairs={{0,1},{1,2},{2,3},{3,4},{4,5},{5,6},{6,7},{8,9},{9,10},{10,11},{11... | collective-permute-start | bytes 1179656 | tf_op jit(solution)/shard_map/ppermute | solution.py:449
  18.6 1.3 %collective-permute-start.1 = (f32[4,2,32,384]{3,2,1,0:T(8,128)S(1)}, f32[4,2,32,384]{3,2,1,0:T(8,128)S(1)}, u32[]{:S(2)}, u32[]{:S(2)}) collective-permute-start(f32[4,2,32,384]{3,2,1,0:T(8,128)S(1)} %all-to-all-done.1.own_ref), channel_id=1, source_target_pairs={{1,0},{2,1},{3,2},{4,3},{5,4},{6,5},{7,6},{9,8},{10,9},{11,10},{12... | collective-permute-start | bytes 1179656 | tf_op jit(solution)/shard_map/ppermute | solution.py:450
  19.9 0.0 copy-done.4
  19.9 17.2 %all_to_all.20.seed_ref = f32[32,8,128]{2,1,0:T(8,128)} all-to-all(f32[32,8,128]{2,1,0:T(8,128)S(1)} %copy-done.4), channel_id=1, replica_groups=mesh['group'=4,'strip'=8] {'group','strip'}, dimensions={0} | all-to-all | bytes 262144 | tf_op jit(solution)/shard_map/all_to_all | solution.py:421
  37.1 2.7 %shard_map.130 = (bf16[128,128]{1,0:T(8,128)(2,1)}, f32[128,512]{1,0:T(8,128)}, f32[128,512]{1,0:T(8,128)}, bf16[128,512]{1,0:T(8,128)(2,1)}, f32[32,8,256]{2,1,0:T(8,128)}) custom-call(f32[32,8,128]{2,1,0:T(8,128)} %all_to_all.20.seed_ref, bf16[128,512]{1,0:T(8,128)(2,1)} %first_ref.1, bf16[512,512]{1,0:T(8,128)(2,1)} %second_ref.3, bf16[512,512]{1,0:T(8,128)(2,1)} %third_ref.3), custom_call_target="tpu_custom_call" | custom-call | tf_op jit(solution)/shard_map/pallas_call | solution.py:291
  39.8 6.5 %shard_map.132.predicted_ref = f32[32,128,256]{2,1,0:T(8,128)} custom-call(bf16[128,512]{1,0:T(8,128)(2,1)} %get-tuple-element.32.hid_ref, bf16[32,512,256]{2,1,0:T(8,128)(2,1)} %shard_map.131.weight_ref), custom_call_target="tpu_custom_call" | custom-call | tf_op jit(solution)/shard_map/pallas_call | solution.py:315
  46.3 0.0 collective-permute-done.top_ref
  46.3 0.0 collective-permute-done.1.bottom_ref
  46.3 0.0 copy-start.3
  46.3 0.0 copy-done
  46.3 0.7 copy-done.2
  47.0 0.2 copy-done.3
  47.2 18.8 %shard_map.133 = (bf16[32,128,256]{2,1,0:T(8,128)(2,1)}, f32[32,8,256]{2,1,0:T(8,128)}) custom-call(s32[1,128]{1,0:T(1,128)} %bitcast.2, f32[4,2,32,384]{3,2,1,0:T(8,128)} %copy-done, f32[4,2,32,384]{3,2,1,0:T(8,128)} %copy-done.2, f32[4,2,32,384]{3,2,1,0:T(8,128)} %copy-done.3, f32[32,128,256]{2,1,0:T(8,128)} %shard_map.132.predicted_ref, ...), custom_call_target="tpu_custom_call" | custom-call | tf_op jit(solution)/shard_map/pallas_call | solution.py:211
  66.0 2.6 %all-to-all-start.2 = ((f32[32,8,256]{2,1,0:T(8,128)}), f32[32,8,256]{2,1,0:T(8,128)S(1)}, u32[]{:S(2)}, u32[]{:S(2)}) async-start(f32[32,8,256]{2,1,0:T(8,128)} %get-tuple-element.34), calls=%async_computation.2 | async-start | bytes 524288 | tf_op jit(solution)/shard_map/all_to_all | solution.py:421
  68.6 8.1 %shard_map.134 = bf16[512,32,256]{2,1,0:T(8,128)(2,1)} custom-call(bf16[128,512]{1,0:T(8,128)(2,1)} %get-tuple-element.32.hid_ref, bf16[32,128,256]{2,1,0:T(8,128)(2,1)} %get-tuple-element.35.res_ref), custom_call_target="tpu_custom_call" | custom-call | flops 1073741824 | bytes 16777216 | tf_op jit(solution)/shard_map/pallas_call | solution.py:343
  76.6 2.3 %all-to-all-done.2.pieces_ref = f32[32,8,256]{2,1,0:T(8,128)S(1)} async-done(((f32[32,8,256]{2,1,0:T(8,128)}), f32[32,8,256]{2,1,0:T(8,128)S(1)}, u32[]{:S(2)}, u32[]{:S(2)}) %all-to-all-start.2) | async-done | bytes 262176 | tf_op jit(solution)/shard_map/all_to_all | solution.py:421
  79.0 0.7 copy-done.1
  79.7 1.7 %shard_map.135 = bf16[32,8,256]{2,1,0:T(8,128)(2,1)} custom-call(s32[1]{0:T(128)} %bitcast.here_ref, f32[32,8,256]{2,1,0:T(8,128)} %copy-done.1, f32[32,8,256]{2,1,0:T(8,128)} %get-tuple-element.37.gate_ref), custom_call_target="tpu_custom_call" | custom-call | tf_op jit(solution)/shard_map/pallas_call | solution.py:373
  81.4 11.8 %all_to_all.21.delta_ref = bf16[32,8,256]{2,1,0:T(8,128)(2,1)} all-to-all(bf16[32,8,256]{2,1,0:T(8,128)(2,1)} %shard_map.135), channel_id=1, replica_groups=mesh['group'=4,'strip'=8] {'group','strip'}, dimensions={0} | all-to-all | bytes 262144 | tf_op jit(solution)/shard_map/all_to_all | solution.py:421
  93.2 3.6 %shard_map.136 = (f32[128,512]{1,0:T(8,128)}, f32[512,512]{1,0:T(8,128)}, f32[512,512]{1,0:T(8,128)}) custom-call(bf16[128,128]{1,0:T(8,128)(2,1)} %get-tuple-element.26.inputs_ref, f32[128,512]{1,0:T(8,128)} %get-tuple-element.27.a_ref, f32[128,512]{1,0:T(8,128)} %get-tuple-element.28.b_ref, bf16[32,8,256]{2,1,0:T(8,128)(2,1)} %all_to_all.21.delta_ref, ...), custom_call_target="tpu_custom_call" | custom-call | tf_op jit(solution)/shard_map/pallas_call | solution.py:406
  (4 shorter events, 0.0 us)
Async XLA Ops:
  3.9 13.2 %all-to-all-start.1 = ((f32[4,2,32,384]{3,2,1,0:T(8,128)}), f32[4,2,32,384]{3,2,1,0:T(8,128)S(1)}, u32[]{:S(2)}, u32[]{:S(2)}) async-start(f32[4,2,32,384]{3,2,1,0:T(8,128)} %get-tuple-element.29), calls=%async_computation.1 | async-start | bytes 786432 | tf_op jit(solution)/shard_map/all_to_all | solution.py:421
  9.1 10.8 %copy-start.4 = (f32[32,8,128]{2,1,0:T(8,128)S(1)}, f32[32,8,128]{2,1,0:T(8,128)}, u32[]{:S(2)}) copy-start(f32[32,8,128]{2,1,0:T(8,128)} %get-tuple-element.25) | copy-start | bytes 393220
  17.1 29.2 %copy-start = (f32[4,2,32,384]{3,2,1,0:T(8,128)}, f32[4,2,32,384]{3,2,1,0:T(8,128)S(1)}, u32[]{:S(2)}) copy-start(f32[4,2,32,384]{3,2,1,0:T(8,128)S(1)} %all-to-all-done.1.own_ref) | copy-start | bytes 1179652
  17.1 29.2 %collective-permute-start = (f32[4,2,32,384]{3,2,1,0:T(8,128)S(1)}, f32[4,2,32,384]{3,2,1,0:T(8,128)S(1)}, u32[]{:S(2)}, u32[]{:S(2)}) collective-permute-start(f32[4,2,32,384]{3,2,1,0:T(8,128)S(1)} %all-to-all-done.1.own_ref), channel_id=1, source_target_pairs={{0,1},{1,2},{2,3},{3,4},{4,5},{5,6},{6,7},{8,9},{9,10},{10,11},{11... | collective-permute-start | bytes 1179656 | tf_op jit(solution)/shard_map/ppermute | solution.py:449
  18.6 27.7 %collective-permute-start.1 = (f32[4,2,32,384]{3,2,1,0:T(8,128)S(1)}, f32[4,2,32,384]{3,2,1,0:T(8,128)S(1)}, u32[]{:S(2)}, u32[]{:S(2)}) collective-permute-start(f32[4,2,32,384]{3,2,1,0:T(8,128)S(1)} %all-to-all-done.1.own_ref), channel_id=1, source_target_pairs={{1,0},{2,1},{3,2},{4,3},{5,4},{6,5},{7,6},{9,8},{10,9},{11,10},{12... | collective-permute-start | bytes 1179656 | tf_op jit(solution)/shard_map/ppermute | solution.py:450
  46.3 0.7 copy-start.2
  46.3 0.9 copy-start.3
  66.0 13.0 %all-to-all-start.2 = ((f32[32,8,256]{2,1,0:T(8,128)}), f32[32,8,256]{2,1,0:T(8,128)S(1)}, u32[]{:S(2)}, u32[]{:S(2)}) async-start(f32[32,8,256]{2,1,0:T(8,128)} %get-tuple-element.34), calls=%async_computation.2 | async-start | bytes 524288 | tf_op jit(solution)/shard_map/all_to_all | solution.py:421
  79.0 0.7 copy-start.1

commit v3 on v2

v3 whole, which is shorter than its diff:
```python
import functools

import jax
import jax.numpy as jnp
from jax import lax
from jax.experimental import pallas as pl
from jax.experimental.pallas import tpu as pltpu
from jax.sharding import PartitionSpec as P

STEPS = 32
LANES = 128
META = 120
step_rate = 0.125

BF16 = jnp.bfloat16
F32 = jnp.float32
ALL = ("group", "strip")
whole = pl.BlockSpec(memory_space=pltpu.VMEM)
scalars = pl.BlockSpec(memory_space=pltpu.SMEM)
far = pl.BlockSpec(memory_space=pl.ANY)


def params(mebibytes):
    return pltpu.CompilerParams(vmem_limit_bytes=mebibytes << 20)


def dot(left, right):
    return jnp.dot(left, right, preferred_element_type=F32)


def contract_rows(left, right):
    return lax.dot_general(left, right, (((0,), (0,)), ((), ())), preferred_element_type=F32)


def contract_cols(left, right):
    return lax.dot_general(left, right, (((1,), (1,)), ((), ())), preferred_element_type=F32)


def lane_tile(c):
    return slice(c * LANES, (c + 1) * LANES)


def tiles_for(cols):
    return -(-(cols + 2 * STEPS) // LANES)


def split_kernel(
    count_ref, emit_ref, field_far, kappa_far, inputs_far, out_ref, seed_ref, field_ref, kappa_ref, inputs_ref, arrived
):
    loads = [
        pltpu.make_async_copy(source, target, arrived.at[i])
        for i, (source, target) in enumerate(
            ((field_far, field_ref), (kappa_far, kappa_ref), (inputs_far, inputs_ref))
        )
    ]
    for load in loads:
        load.start()
    blocks, _, rows, width = out_ref.shape
    tiles = width // LANES
    total = field_ref.shape[2]
    cols = total // blocks
    span = cols + 2 * LANES
    source = lax.broadcasted_iota(jnp.int32, (span, width), 0) - (LANES - STEPS)
    place = lax.broadcasted_iota(jnp.int32, (span, width), 1)
    wanted = tiles * (place % LANES) + place // LANES
    deal = ((source == wanted) & (wanted < cols + 2 * STEPS)).astype(F32).astype(BF16)
    for load in loads:
        load.wait()
    none = jnp.zeros((2 * rows, LANES), F32)
    both = jnp.concatenate([field_ref[0], kappa_ref[0] * step_rate], axis=0)
    both = jnp.concatenate([none, both, none], axis=1)
    high = both.astype(BF16)
    rest = both - high.astype(F32)
    middle = rest.astype(BF16)
    low = (rest - middle.astype(F32)).astype(BF16)
    lane = lax.broadcasted_iota(jnp.int32, (rows, LANES), 1)
    row = lax.broadcasted_iota(jnp.int32, (rows, LANES), 0)
    meta = jnp.zeros((rows, LANES), F32)
    for s in range(emit_ref.shape[1]):
        last = jnp.minimum(emit_ref[0, s], count_ref[0]) - 1
        meta = jnp.where(row == s, last.astype(F32), meta)
    windows = [slice(g * cols, g * cols + span) for g in range(blocks)]
    stacked = [part[:, window] for window in windows for part in (high, middle, low)]
    product = dot(jnp.concatenate(stacked, axis=0), deal)
    for g in range(blocks):
        parts = [product[2 * rows * (3 * g + i) : 2 * rows * (3 * g + i + 1)] for i in range(3)]
        dealt = parts[0] + parts[1] + parts[2]
        out_ref[g, 0] = dealt[:rows]
        out_ref[g, 1] = dealt[rows:]
        out_ref[g, 0, :, :LANES] = jnp.where(lane == META, meta, dealt[:rows, :LANES])
    here = inputs_ref.shape[0]
    devices, deep, features = seed_ref.shape
    seed = inputs_ref[...].astype(F32)
    if deep > here:
        seed = jnp.concatenate([seed, jnp.zeros((deep - here, features), F32)], axis=0)
    for d in range(devices):
        seed_ref[d] = seed


def split_columns(initial, conductivity, step_count, emit_steps, inputs, blocks, devices):
    _, rows, total = initial.shape
    width = tiles_for(total // blocks) * LANES
    here, features = inputs.shape
    return pl.pallas_call(
        split_kernel,
        in_specs=[scalars, scalars, far, far, far],
        out_specs=[whole, whole],
        out_shape=[
            jax.ShapeDtypeStruct((blocks, 2, rows, width), F32),
            jax.ShapeDtypeStruct((devices, -(-here // 8) * 8, features), F32),
        ],
        scratch_shapes=[
            pltpu.VMEM(initial.shape, F32),
            pltpu.VMEM(conductivity.shape, F32),
            pltpu.VMEM(inputs.shape, BF16),
            pltpu.SemaphoreType.DMA((3,)),
        ],
        compiler_params=params(63),
    )(step_count, emit_steps, initial, conductivity, inputs)


def advance(state, rate, history, pitch, part, fields, now, t):
    _, _, tiles, depth, _ = state.shape
    rows = (depth - 16) // 3
    later = 1 - now
    for tile in range(part, 3 * rows // 8 - part):
        a = 8 + 8 * tile
        for f in fields:
            middle = [state[f, now, j, a : a + 8, :] for j in range(tiles)]
            west = [pltpu.roll(middle[-1], 1, 1)] + middle[:-1]
            east = middle[1:] + [pltpu.roll(middle[0], LANES - 1, 1)]
            for j in range(tiles):
                north = state[f, now, j, a - 1 : a + 7, :]
                south = state[f, now, j, a + 1 : a + 9, :]
                beside = (north + south) + (west[j] + east[j])
                gain = rate[f, j, a : a + 8, :] * (1.0 + 0.25 * jnp.tanh(middle[j]))
                value = middle[j] + gain * (beside - 4.0 * middle[j])
                state[f, later, j, a : a + 8, :] = value
                if rows <= 8 * tile < 2 * rows:
                    start = (8 * tile - rows) * pitch + f * STEPS + t
                    history[j, pl.ds(start, 8, stride=pitch), :] = value


def fold_rows(value, out_ref):
    devices, deep, folded = out_ref.shape
    batch, units = value.shape
    here = batch // devices
    for d in range(devices):
        for k in range(units // folded):
            out_ref[d, k * here : (k + 1) * here, :] = value[
                d * here : (d + 1) * here, k * folded : (k + 1) * folded
            ]


def by_row_kernel(first, weight_far, out_far, weight, by_rows, arrived, left):
    pieces, units, rows, cols = weight.shape
    places = [slice(i * units, (i + 1) * units) for i in range(pieces)]
    sources = [slice(first + i * units, first + (i + 1) * units) for i in range(pieces)]
    loads = [
        pltpu.make_async_copy(weight_far.at[sources[i]], weight.at[i], arrived.at[i])
        for i in range(pieces)
    ]
    stores = [
        pltpu.make_async_copy(by_rows.at[i], out_far.at[:, places[i], :], left.at[i])
        for i in range(pieces)
    ]
    for load in loads:
        load.start()
    for i in range(pieces):
        loads[i].wait()

        def some_units(u, _):
            place = pl.ds(pl.multiple_of(u * 16, 16), 16)
            for c in range(cols // LANES):
                for r in range(0, rows, 16):
                    block = weight[i, place, r : r + 16, lane_tile(c)]
                    by_rows[i, r : r + 16, place, lane_tile(c)] = jnp.swapaxes(block, 0, 1)
            return 0

        lax.fori_loop(0, units // 16, some_units, 0)
        stores[i].start()
    for store in stores:
        store.wait()


def by_row(weight, half, pieces=4):
    units, rows, cols = weight.shape
    units = units // 2
    return pl.pallas_call(
        functools.partial(by_row_kernel, half * units),
        in_specs=[far],
        out_specs=far,
        out_shape=jax.ShapeDtypeStruct((rows, units, cols), BF16),
        scratch_shapes=[
            pltpu.VMEM((pieces, units // pieces, rows, cols), BF16),
            pltpu.VMEM((pieces, rows, units // pieces, cols), BF16),
            pltpu.SemaphoreType.DMA((pieces,)),
            pltpu.SemaphoreType.DMA((pieces,)),
        ],
        compiler_params=params(63),
        cost_estimate=pl.CostEstimate(
            flops=0, bytes_accessed=4 * units * rows * cols, transcendentals=0
        ),
    )(weight)


def forward(seed_ref, first_ref, second_ref, third_ref, inputs, act_a, act_b, hidden, gate, raw, scratch):
    devices = seed_ref.shape[0]
    here = inputs.shape[0] // devices
    for d in range(devices):
        raw[d * here : (d + 1) * here, :] = seed_ref[d, :here, :]
    inputs[...] = raw[...].astype(BF16)
    act = jnp.tanh(dot(inputs[...], first_ref[...]))
    act_a[...] = act
    act = jnp.tanh(dot(act.astype(BF16), second_ref[...]))
    act_b[...] = act
    act = jnp.tanh(dot(act.astype(BF16), third_ref[...]))
    hidden[...] = act.astype(BF16)
    scratch[...] = 1.0 - act * act
    fold_rows(scratch, gate)


def main_kernel(
    scale, snaps, own_far, top_far, bottom_far, seed_far, low_far, high_far, assign_far, first_far, second_far, third_far,
    res_far, back_ref, in_far, a_far, b_far, hid_far, gate_far,
    state, rate, history, picked, predicted, by_rows, total, raw, assigned, first, second, third,
    own_ref, top_ref, bottom_ref, seed_ref, res, inputs, act_a, act_b, hidden, gate, arrived, filled, left,
):
    fields, _, rows, width = own_ref.shape
    _, batch, cols = predicted.shape
    units = by_rows.shape[1]
    tiles = width // LANES
    entries = fields * STEPS
    pitch = entries + 1
    pairs = (
        (seed_far, seed_ref), (first_far, first), (second_far, second), (third_far, third),
        (top_far, top_ref), (own_far, own_ref), (bottom_far, bottom_ref), (assign_far, assigned),
    )
    loads = [
        pltpu.make_async_copy(source, target, arrived.at[i])
        for i, (source, target) in enumerate(pairs)
    ]
    for load in loads:
        load.start()
    together = 2 if fields % 2 == 0 else 1
    parts = STEPS // 8
    turns = fields // together * parts
    each = -(-rows // (4 * turns))
    fills = [
        [
            pltpu.make_async_copy(
                source.at[low : low + 4 * each],
                by_rows.at[low : low + 4 * each, half * units // 2 : (half + 1) * units // 2, :],
                filled.at[half, low // (4 * each)],
            )
            for half, source in enumerate((low_far, high_far))
        ]
        for low in range(0, rows, 4 * each)
    ]
    for pair in fills:
        for fill in pair:
            fill.start()
    for load in loads[:4]:
        load.wait()
    forward(seed_ref, first, second, third, inputs, act_a, act_b, hidden, gate, raw, total)
    stores = [
        pltpu.make_async_copy(source, target, left.at[i])
        for i, (source, target) in enumerate(
            ((inputs, in_far), (act_a, a_far), (act_b, b_far), (hidden, hid_far), (gate, gate_far))
        )
    ]
    for store in stores:
        store.start()
    for load in loads[4:]:
        load.wait()

    for f in range(fields):
        for now in range(2):
            for j in range(tiles):
                state[f, now, j, :8, :] = jnp.zeros((8, LANES), F32)
                state[f, now, j, 8 + 3 * rows :, :] = jnp.zeros((8, LANES), F32)
        for j in range(tiles):
            for place, ref in enumerate((top_ref, own_ref, bottom_ref)):
                low = 8 + place * rows
                state[f, 0, j, low : low + rows, :] = ref[f, 0, :, lane_tile(j)]
                rate[f, j, low : low + rows, :] = ref[f, 1, :, lane_tile(j)]
                if place != 1:
                    state[f, 1, j, low : low + rows, :] = ref[f, 0, :, lane_tile(j)]
    for turn in range(turns):
        if turn < len(fills):
            for fill in fills[turn]:
                fill.wait()
        which = [turn // parts * together + i for i in range(together)]
        part = turn % parts

        def two_steps(pair, _):
            for now in range(2):
                advance(state, rate, history, pitch, part, which, now, 2 * pair + now)
            if turn * 4 * each < rows:
                for k in range(each):
                    r = (turn * 4 + pair - 4 * part) * each + k
                    predicted[r] = dot(hidden[...], by_rows[r])
            return 0

        lax.fori_loop(4 * part, 4 * part + 4, two_steps, 0)

    lane = lax.broadcasted_iota(jnp.int32, (snaps, entries), 1)
    steps = []
    for f in range(fields):
        last = own_ref[f, 0, :snaps, META : META + 1].astype(jnp.int32)
        steps.append((lane == f * STEPS + last).astype(F32))
    steps = jnp.concatenate(steps, axis=0).astype(BF16)
    number = lax.broadcasted_iota(jnp.int32, (fields * snaps, batch), 0)
    chosen = (number == assigned[...]).astype(F32).astype(BF16)
    hot = contract_rows(chosen, steps).astype(BF16)
    place = lax.broadcasted_iota(jnp.int32, (width, cols), 0)
    column = lax.broadcasted_iota(jnp.int32, (width, cols), 1) + STEPS
    gather = (tiles * (place % LANES) + place // LANES == column).astype(F32).astype(BF16)

    chunk = 8
    for i in range(rows // chunk):
        for k in range(chunk):
            low = (i * chunk + k) * pitch
            for j in range(tiles):
                states = history[j, low : low + entries, :].astype(BF16)
                picked[k * batch : (k + 1) * batch, lane_tile(j)] = dot(hot, states).astype(BF16)
        targets = dot(picked[...], gather)
        back = None
        for k in range(chunk):
            r = i * chunk + k
            residual = ((predicted[r] - targets[k * batch : (k + 1) * batch]) * scale).astype(BF16)
            res[r] = residual
            part = contract_cols(residual, by_rows[r])
            back = part if back is None else back + part
        total[...] = back if i == 0 else total[...] + back
        place = slice(i * chunk, (i + 1) * chunk)
        stores.append(pltpu.make_async_copy(res.at[place], res_far.at[place], left.at[5 + i]))
        stores[-1].start()
    fold_rows(total, back_ref)
    for store in stores:
        store.wait()


def main(assign, own, top, bottom, seeds, w_first, w_second, w_third, halves, snaps, here, fold):
    rows, units, cols = halves[0].shape
    units = 2 * units
    features = w_first.shape[0]
    devices = seeds.shape[0]
    batch = devices * here
    fields, _, _, width = own.shape
    tiles = width // LANES
    depth = 3 * rows + 16
    entries = fields * STEPS
    scale = 1.0 / float(batch) ** 0.5
    folded = (devices, here * fold, units // fold)
    kept = [
        ((rows, batch, cols), BF16),
        ((batch, features), BF16),
        ((batch, units), F32),
        ((batch, units), F32),
        ((batch, units), BF16),
        (folded, F32),
    ]
    shapes = [jax.ShapeDtypeStruct(*k) for k in kept]
    return pl.pallas_call(
        functools.partial(main_kernel, scale, snaps),
        in_specs=[far] * 10,
        out_specs=[far, whole] + [far] * 5,
        out_shape=[shapes[0], jax.ShapeDtypeStruct(folded, F32)] + shapes[1:],
        scratch_shapes=[
            pltpu.VMEM((fields, 2, tiles, depth, LANES), F32),
            pltpu.VMEM((fields, tiles, depth, LANES), F32),
            pltpu.VMEM((tiles, rows * (entries + 1), LANES), F32),
            pltpu.VMEM((8 * batch, width), BF16),
            pltpu.VMEM((rows, batch, cols), F32),
            pltpu.VMEM((rows, units, cols), BF16),
            pltpu.VMEM((batch, units), F32),
            pltpu.VMEM((batch, features), F32),
            pltpu.VMEM((1, batch), jnp.int32),
            pltpu.VMEM(w_first.shape, BF16),
            pltpu.VMEM(w_second.shape, BF16),
            pltpu.VMEM(w_third.shape, BF16),
            pltpu.VMEM(own.shape, F32),
            pltpu.VMEM(own.shape, F32),
            pltpu.VMEM(own.shape, F32),
            pltpu.VMEM(seeds.shape, F32),
        ]
        + [pltpu.VMEM(*k) for k in kept]
        + [
            pltpu.SemaphoreType.DMA((8,)),
            pltpu.SemaphoreType.DMA((2, rows // 4)),
            pltpu.SemaphoreType.DMA((5 + rows // 8,)),
        ],
        compiler_params=params(63),
    )(own, top, bottom, seeds, *halves, assign.reshape(1, batch), w_first, w_second, w_third)


def outer_kernel(hid_ref, res_ref, out_ref, grads):
    rows, _, cols = res_ref.shape
    units = out_ref.shape[0]
    for r in range(rows):
        grads[r] = contract_rows(hid_ref[...], res_ref[r]).astype(BF16)
    for c in range(cols // LANES):
        for u in range(0, units, 16):
            for r in range(0, rows, 16):
                block = grads[r : r + 16, u : u + 16, lane_tile(c)]
                out_ref[u : u + 16, r : r + 16, lane_tile(c)] = jnp.swapaxes(block, 0, 1)


def outer(hidden, res, chunk=128):
    rows, batch, cols = res.shape
    units = hidden.shape[1]
    return pl.pallas_call(
        outer_kernel,
        grid=(units // chunk,),
        in_specs=[
            pl.BlockSpec((batch, chunk), lambda i: (0, i)),
            pl.BlockSpec((rows, batch, cols), lambda i: (0, 0, 0)),
        ],
        out_specs=pl.BlockSpec((chunk, rows, cols), lambda i: (i, 0, 0)),
        out_shape=jax.ShapeDtypeStruct((units, rows, cols), BF16),
        scratch_shapes=[pltpu.VMEM((rows, chunk, cols), BF16)],
        compiler_params=params(63),
        cost_estimate=pl.CostEstimate(
            flops=2 * batch * units * rows * cols,
            bytes_accessed=4 * units * rows * cols,
            transcendentals=0,
        ),
    )(hidden, res)


def delta_kernel(pieces_far, gate_far, out_ref, pieces, gate, arrived):
    devices = pieces.shape[0]
    loads = [
        pltpu.make_async_copy(pieces_far, pieces, arrived.at[0]),
        pltpu.make_async_copy(gate_far.at[lax.axis_index(ALL)], gate, arrived.at[1]),
    ]
    for load in loads:
        load.start()
    for load in loads:
        load.wait()
    back = [pieces[d] for d in range(devices)]
    while len(back) > 1:
        back = [a + b for a, b in zip(back[::2], back[1::2])] + back[len(back) // 2 * 2 :]
    delta = (back[0] * gate[...]).astype(BF16)
    for d in range(devices):
        out_ref[d] = delta


def delta_spread(pieces, gate):
    return pl.pallas_call(
        delta_kernel,
        in_specs=[far, far],
        out_specs=whole,
        out_shape=jax.ShapeDtypeStruct(pieces.shape, BF16),
        scratch_shapes=[
            pltpu.VMEM(pieces.shape, F32),
            pltpu.VMEM(gate.shape[1:], F32),
            pltpu.SemaphoreType.DMA((2,)),
        ],
        compiler_params=params(63),
    )(pieces, gate)


def backward_kernel(
    inputs_far, a_far, b_far, delta_far, second_far, third_far, g1_far, g2_far, g3_far,
    inputs, act_a, act_b, folded, second, third, wide, unfolded, g1, g2, g3, arrived, left,
):
    pairs = (
        (delta_far, folded), (b_far, act_b), (third_far, third),
        (a_far, act_a), (second_far, second), (inputs_far, inputs),
    )
    loads = [
        pltpu.make_async_copy(source, target, arrived.at[i])
        for i, (source, target) in enumerate(pairs)
    ]
    for load in loads:
        load.start()
    stores = [
        pltpu.make_async_copy(source, target, left.at[i])
        for i, (source, target) in enumerate(((g3, g3_far), (g2, g2_far), (g1, g1_far)))
    ]
    devices, deep, width = folded.shape
    batch, units = act_a.shape
    here = batch // devices
    loads[0].wait()
    wide[...] = folded[...].astype(F32)
    for d in range(devices):
        for k in range(units // width):
            unfolded[d * here : (d + 1) * here, k * width : (k + 1) * width] = wide[
                d, k * here : (k + 1) * here, :
            ]
    delta = unfolded[...].astype(BF16)
    loads[1].wait()
    act = act_b[...]
    g3[...] = contract_rows(act.astype(BF16), delta)
    stores[0].start()
    loads[2].wait()
    delta = (contract_cols(delta, third[...]) * (1.0 - act * act)).astype(BF16)
    loads[3].wait()
    act = act_a[...]
    g2[...] = contract_rows(act.astype(BF16), delta)
    stores[1].start()
    loads[4].wait()
    delta = (contract_cols(delta, second[...]) * (1.0 - act * act)).astype(BF16)
    loads[5].wait()
    g1[...] = contract_rows(inputs[...], delta)
    stores[2].start()
    for store in stores:
        store.wait()


def backward(inputs, act_a, act_b, delta, w_second, w_third):
    batch, units = act_a.shape
    shapes = [(inputs.shape[1], units), (units, units), (units, units)]
    return pl.pallas_call(
        backward_kernel,
        in_specs=[far] * 6,
        out_specs=[far] * 3,
        out_shape=[jax.ShapeDtypeStruct(shape, F32) for shape in shapes],
        scratch_shapes=[
            pltpu.VMEM(inputs.shape, BF16),
            pltpu.VMEM(act_a.shape, F32),
            pltpu.VMEM(act_b.shape, F32),
            pltpu.VMEM(delta.shape, BF16),
            pltpu.VMEM(w_second.shape, BF16),
            pltpu.VMEM(w_third.shape, BF16),
            pltpu.VMEM(delta.shape, F32),
            pltpu.VMEM((batch, units), F32),
        ]
        + [pltpu.VMEM(shape, F32) for shape in shapes]
        + [pltpu.SemaphoreType.DMA((6,)), pltpu.SemaphoreType.DMA((3,))],
        compiler_params=params(63),
    )(inputs, act_a, act_b, delta, w_second, w_third)


def swap(value, axes):
    return lax.all_to_all(value, axes, split_axis=0, concat_axis=0, tiled=True)


def per_device(
    initial,
    conductivity,
    step_count,
    emit_steps,
    assign,
    sample_inputs,
    w_first,
    w_second,
    w_third,
    w_out,
):
    groups, strips = lax.axis_size("group"), lax.axis_size("strip")
    devices = groups * strips
    here = sample_inputs.shape[0]
    fold = max(1, 8 // here)
    blocks, seeds = split_columns(
        initial, conductivity, step_count, emit_steps, sample_inputs, groups, devices
    )
    blocks, w_out = lax.optimization_barrier((blocks, w_out))
    own = swap(blocks, "group")
    low = by_row(w_out, 0)
    own, low, w_out = lax.optimization_barrier((own, low, w_out))
    down = [(i, i + 1) for i in range(strips - 1)]
    top = lax.ppermute(own, "strip", down)
    bottom = lax.ppermute(own, "strip", [(j, i) for i, j in down])
    own, seeds = lax.optimization_barrier((own, seeds))
    seeds = swap(seeds, ALL)
    res, partial, inputs, act_a, act_b, hidden, gate = main(
        assign, own, top, bottom, seeds, w_first, w_second, w_third, (low, by_row(w_out, 1)),
        emit_steps.shape[1], here, fold,
    )
    pieces = swap(partial, ALL)
    grad_out = outer(hidden, res)
    pieces, grad_out = lax.optimization_barrier((pieces, grad_out))
    delta = swap(delta_spread(pieces, gate), ALL)
    grads = backward(inputs, act_a, act_b, delta, w_second, w_third)
    return (*grads, grad_out)


def solution(mesh):
    placed = (
        P("group", "strip", None),
        P("group", "strip", None),
        P("group"),
        P("group", None),
        P(),
        P(("group", "strip"), None),
        P(),
        P(),
        P(),
        P(None, "strip", "group"),
    )
    return jax.shard_map(
        per_device,
        mesh=mesh,
        in_specs=placed,
        out_specs=(P(), P(), P(), P(None, "strip", "group")),
        check_vma=False,
    )
```

time: 97.4 us -> 83.4 us (0.86)
  blocking collectives: 29 us -> 11.8 us
  Pallas kernels: 52 us -> 41.5 us
  waiting for transfers between devices: 2.33 us -> 9.73 us
  starting transfers between devices: 10.5 us -> 17 us
    all_to_all x2 -> x1, blocking collectives: 29 us -> 11.8 us  [swap(): return lax.all_to_all(value, axes, split_axis=0, concat_axis=0, tiled=True)]
    pallas_call x7 -> x6, Pallas kernels: 44 us -> 33.4 us  [the longest x1 18.2 us: main(): pl.pallas_call(functools.partial(main_kernel, scale, snaps), in_specs=[fa...]
    all_to_all x2 -> x3, waiting for transfers between devices: 2.33 us -> 9.72 us  [swap(): return lax.all_to_all(value, axes, split_axis=0, concat_axis=0, tiled=True)]
    all_to_all x2 -> x3, starting transfers between devices: 7.76 us -> 11.9 us  [swap(): return lax.all_to_all(value, axes, split_axis=0, concat_axis=0, tiled=True)]
    ppermute x1, starting transfers between devices: 1.47 us -> 3.81 us  [per_device(): top = lax.ppermute(own, 'strip', down)]
  transfers between devices with their start and end apart: 4 -> 5, of which waited for: 1 -> 3; matrix products, arithmetic and copies ran while one was open for 0% -> 0% of each run, Pallas kernels for 26% -> 19%
where the time goes in v3:
time: 83.4 us; the launch traced here: 82.9 us
  Pallas kernels  41.5 us (50%)
  starting transfers between devices  17 us (20%)
  blocking collectives  11.8 us (14%)
  waiting for transfers between devices  9.73 us (12%)
  local copies, waits for them, and re-layouts  1.48 us (2%)
  between operations  1.36 us (2%)
    pallas_call x1, Pallas kernels, main(): pl.pallas_call(functools.partial(main_kernel, scale, snaps), in_specs=[fa...  18.2 us
    all_to_all x3, starting transfers between devices, swap(): return lax.all_to_all(value, axes, split_axis=0, concat_axis=0, tiled=True)  11.9 us
    all_to_all x1, blocking collectives, swap(): return lax.all_to_all(value, axes, split_axis=0, concat_axis=0, tiled=True)  11.8 us
    all_to_all x3, waiting for transfers between devices, swap(): return lax.all_to_all(value, axes, split_axis=0, concat_axis=0, tiled=True)  9.72 us
    pallas_call x1, Pallas kernels, outer(): pl.pallas_call(outer_kernel, grid=(units // chunk,), in_specs=[pl.BlockSp...  8.05 us
    pallas_call x2, Pallas kernels, by_row(): pl.pallas_call(functools.partial(by_row_kernel, half * units), in_specs=[...  7.37 us
    ppermute x1, starting transfers between devices, per_device(): top = lax.ppermute(own, 'strip', down)  3.81 us
    pallas_call x1, Pallas kernels, backward(): pl.pallas_call(backward_kernel, in_specs=[far] * 6, out_specs=[far] * 3,...  3.26 us
  transfers between devices with their start and end apart: 5, of which 3 were waited for; matrix products, arithmetic and copies ran while one was open for 0% of the time, Pallas kernels for 19%

profile of v3, /device:TPU:0, one launch (start us, length us, event | category | flops | bytes accessed | tf_op | source)
XLA Modules:
  0.0 82.9 jit_solution(9897728348056353630)
XLA Ops:
  1.3 3.0 %shard_map.129 = (f32[4,2,32,384]{3,2,1,0:T(8,128)}, f32[32,8,128]{2,1,0:T(8,128)}) custom-call(s32[1]{0:T(128)S(6)} %copy.14.count_ref, s32[1,16]{1,0:T(1,128)} %emit_ref.1, f32[1,32,1024]{2,1,0:T(8,128)} %field_far.1, f32[1,32,1024]{2,1,0:T(8,128)} %kappa_far.1, bf16[4,128]{1,0:T(4,128)(2,1)} %inputs_far.1), custom_call_target="tpu_custom_call" | custom-call | tf_op jit(solution)/shard_map/pallas_call | solution.py:104
  4.3 5.2 %all-to-all-start = ((f32[4,2,32,384]{3,2,1,0:T(8,128)}), f32[4,2,32,384]{3,2,1,0:T(8,128)S(1)}, u32[]{:S(2)}, u32[]{:S(2)}) async-start(f32[4,2,32,384]{3,2,1,0:T(8,128)} %get-tuple-element.26), calls=%async_computation | async-start | bytes 786432 | tf_op jit(solution)/shard_map/all_to_all | solution.py:538
  9.4 3.7 %shard_map.130.low_far = bf16[32,256,256]{2,1,0:T(8,128)(2,1)} custom-call(bf16[512,32,256]{2,1,0:T(8,128)(2,1)} %weight_far.1), custom_call_target="tpu_custom_call" | custom-call | bytes 8388608 | tf_op jit(solution)/shard_map/pallas_call | solution.py:189
  13.1 3.0 %all-to-all-done.own_far = f32[4,2,32,384]{3,2,1,0:T(8,128)S(1)} async-done(((f32[4,2,32,384]{3,2,1,0:T(8,128)}), f32[4,2,32,384]{3,2,1,0:T(8,128)S(1)}, u32[]{:S(2)}, u32[]{:S(2)}) %all-to-all-start) | async-done | bytes 393248 | tf_op jit(solution)/shard_map/all_to_all | solution.py:538
  16.1 1.3 %collective-permute-start.1 = (f32[4,2,32,384]{3,2,1,0:T(8,128)S(1)}, f32[4,2,32,384]{3,2,1,0:T(8,128)S(1)}, u32[]{:S(2)}, u32[]{:S(2)}) collective-permute-start(f32[4,2,32,384]{3,2,1,0:T(8,128)S(1)} %all-to-all-done.own_far), channel_id=1, source_target_pairs={{1,0},{2,1},{3,2},{4,3},{5,4},{6,5},{7,6},{9,8},{10,9},{11,10},{12... | collective-permute-start | bytes 1179656 | tf_op jit(solution)/shard_map/ppermute | solution.py:566
  17.3 3.8 %collective-permute-start = (f32[4,2,32,384]{3,2,1,0:T(8,128)S(1)}, f32[4,2,32,384]{3,2,1,0:T(8,128)}, u32[]{:S(2)}, u32[]{:S(2)}) collective-permute-start(f32[4,2,32,384]{3,2,1,0:T(8,128)S(1)} %all-to-all-done.own_far), channel_id=1, source_target_pairs={{0,1},{1,2},{2,3},{3,4},{4,5},{5,6},{6,7},{8,9},{9,10},{10,11},{11... | collective-permute-start | bytes 1179656 | tf_op jit(solution)/shard_map/ppermute | solution.py:565
  21.2 4.1 %all-to-all-start.1 = ((f32[32,8,128]{2,1,0:T(8,128)}), f32[32,8,128]{2,1,0:T(8,128)S(1)}, u32[]{:S(2)}, u32[]{:S(2)}) async-start(f32[32,8,128]{2,1,0:T(8,128)} %get-tuple-element.31), calls=%async_computation.1 | async-start | bytes 262144 | tf_op jit(solution)/shard_map/all_to_all | solution.py:538
  25.3 3.7 %shard_map.131.high_far = bf16[32,256,256]{2,1,0:T(8,128)(2,1)} custom-call(bf16[512,32,256]{2,1,0:T(8,128)(2,1)} %weight_far.1), custom_call_target="tpu_custom_call" | custom-call | bytes 8388608 | tf_op jit(solution)/shard_map/pallas_call | solution.py:189
  29.0 0.0 copy-done
  29.0 4.4 %all-to-all-done.1.seed_far = f32[32,8,128]{2,1,0:T(8,128)S(1)} async-done(((f32[32,8,128]{2,1,0:T(8,128)}), f32[32,8,128]{2,1,0:T(8,128)S(1)}, u32[]{:S(2)}, u32[]{:S(2)}) %all-to-all-start.1) | async-done | bytes 131104 | tf_op jit(solution)/shard_map/all_to_all | solution.py:538
  33.5 0.0 copy-start.2
  33.5 0.0 collective-permute-done.1.bottom_far
  33.5 0.0 copy-start.3
  33.5 0.0 collective-permute-done.top_far
  33.5 0.6 copy-done.2
  34.1 0.1 copy-done.3
  34.3 18.2 %shard_map.132 = (bf16[32,128,256]{2,1,0:T(8,128)(2,1)}, f32[32,8,256]{2,1,0:T(8,128)}, bf16[128,128]{1,0:T(8,128)(2,1)}, f32[128,512]{1,0:T(8,128)}, f32[128,51...) custom-call(f32[4,2,32,384]{3,2,1,0:T(8,128)} %copy-done, ...), custom_call_target="tpu_custom_call" | custom-call | tf_op jit(solution)/shard_map/pallas_call | solution.py:365
  52.4 2.6 %all-to-all-start.2 = ((f32[32,8,256]{2,1,0:T(8,128)}), f32[32,8,256]{2,1,0:T(8,128)S(1)}, u32[]{:S(2)}, u32[]{:S(2)}) async-start(f32[32,8,256]{2,1,0:T(8,128)} %get-tuple-element.37), calls=%async_computation.2 | async-start | bytes 524288 | tf_op jit(solution)/shard_map/all_to_all | solution.py:538
  55.1 8.1 %shard_map.133 = bf16[512,32,256]{2,1,0:T(8,128)(2,1)} custom-call(bf16[128,512]{1,0:T(8,128)(2,1)} %get-tuple-element.38.hid_ref, bf16[32,128,256]{2,1,0:T(8,128)(2,1)} %get-tuple-element.39.res_ref), custom_call_target="tpu_custom_call" | custom-call | flops 1073741824 | bytes 16777216 | tf_op jit(solution)/shard_map/pallas_call | solution.py:413
  63.1 2.3 %all-to-all-done.2.pieces_far = f32[32,8,256]{2,1,0:T(8,128)S(1)} async-done(((f32[32,8,256]{2,1,0:T(8,128)}), f32[32,8,256]{2,1,0:T(8,128)S(1)}, u32[]{:S(2)}, u32[]{:S(2)}) %all-to-all-start.2) | async-done | bytes 262176 | tf_op jit(solution)/shard_map/all_to_all | solution.py:538
  65.4 0.7 copy-done.1
  66.1 1.6 %shard_map.134 = bf16[32,8,256]{2,1,0:T(8,128)(2,1)} custom-call(f32[32,8,256]{2,1,0:T(8,128)} %copy-done.1, f32[32,8,256]{2,1,0:T(8,128)} %get-tuple-element.41.gate_far), custom_call_target="tpu_custom_call" | custom-call | tf_op jit(solution)/shard_map/pallas_call | solution.py:451
  67.8 11.8 %all_to_all.20.delta_far = bf16[32,8,256]{2,1,0:T(8,128)(2,1)} all-to-all(bf16[32,8,256]{2,1,0:T(8,128)(2,1)} %shard_map.134), channel_id=1, replica_groups=mesh['group'=4,'strip'=8] {'group','strip'}, dimensions={0} | all-to-all | bytes 262144 | tf_op jit(solution)/shard_map/all_to_all | solution.py:538
  79.6 3.3 %shard_map.135 = (f32[128,512]{1,0:T(8,128)}, f32[512,512]{1,0:T(8,128)}, f32[512,512]{1,0:T(8,128)}) custom-call(bf16[128,128]{1,0:T(8,128)(2,1)} %get-tuple-element.34.inputs_far, f32[128,512]{1,0:T(8,128)} %get-tuple-element.35.a_far, f32[128,512]{1,0:T(8,128)} %get-tuple-element.36.b_far, bf16[32,8,256]{2,1,0:T(8,128)(2,1)} %all_to_all.20.delta_far, ...), custom_call_target="tpu_custom_call" | custom-call | tf_op jit(solution)/shard_map/pallas_call | solution.py:516
  (2 shorter events, 0.0 us)
Async XLA Ops:
  4.3 11.8 %all-to-all-start = ((f32[4,2,32,384]{3,2,1,0:T(8,128)}), f32[4,2,32,384]{3,2,1,0:T(8,128)S(1)}, u32[]{:S(2)}, u32[]{:S(2)}) async-start(f32[4,2,32,384]{3,2,1,0:T(8,128)} %get-tuple-element.26), calls=%async_computation | async-start | bytes 786432 | tf_op jit(solution)/shard_map/all_to_all | solution.py:538
  16.1 13.0 %copy-start = (f32[4,2,32,384]{3,2,1,0:T(8,128)}, f32[4,2,32,384]{3,2,1,0:T(8,128)S(1)}, u32[]{:S(2)}) copy-start(f32[4,2,32,384]{3,2,1,0:T(8,128)S(1)} %all-to-all-done.own_far) | copy-start | bytes 1179652
  16.1 17.4 %collective-permute-start.1 = (f32[4,2,32,384]{3,2,1,0:T(8,128)S(1)}, f32[4,2,32,384]{3,2,1,0:T(8,128)S(1)}, u32[]{:S(2)}, u32[]{:S(2)}) collective-permute-start(f32[4,2,32,384]{3,2,1,0:T(8,128)S(1)} %all-to-all-done.own_far), channel_id=1, source_target_pairs={{1,0},{2,1},{3,2},{4,3},{5,4},{6,5},{7,6},{9,8},{10,9},{11,10},{12... | collective-permute-start | bytes 1179656 | tf_op jit(solution)/shard_map/ppermute | solution.py:566
  17.3 16.1 %collective-permute-start = (f32[4,2,32,384]{3,2,1,0:T(8,128)S(1)}, f32[4,2,32,384]{3,2,1,0:T(8,128)}, u32[]{:S(2)}, u32[]{:S(2)}) collective-permute-start(f32[4,2,32,384]{3,2,1,0:T(8,128)S(1)} %all-to-all-done.own_far), channel_id=1, source_target_pairs={{0,1},{1,2},{2,3},{3,4},{4,5},{5,6},{6,7},{8,9},{9,10},{10,11},{11... | collective-permute-start | bytes 1179656 | tf_op jit(solution)/shard_map/ppermute | solution.py:565
  21.2 12.3 %all-to-all-start.1 = ((f32[32,8,128]{2,1,0:T(8,128)}), f32[32,8,128]{2,1,0:T(8,128)S(1)}, u32[]{:S(2)}, u32[]{:S(2)}) async-start(f32[32,8,128]{2,1,0:T(8,128)} %get-tuple-element.31), calls=%async_computation.1 | async-start | bytes 262144 | tf_op jit(solution)/shard_map/all_to_all | solution.py:538
  33.5 0.6 copy-start.2
  33.5 0.8 copy-start.3
  52.4 13.0 %all-to-all-start.2 = ((f32[32,8,256]{2,1,0:T(8,128)}), f32[32,8,256]{2,1,0:T(8,128)S(1)}, u32[]{:S(2)}, u32[]{:S(2)}) async-start(f32[32,8,256]{2,1,0:T(8,128)} %get-tuple-element.37), calls=%async_computation.2 | async-start | bytes 524288 | tf_op jit(solution)/shard_map/all_to_all | solution.py:538
  65.4 0.7 copy-start.1

commit v4 on v3

--- a/solution.py
+++ b/solution.py
@@ -20,8 +20,8 @@
 far = pl.BlockSpec(memory_space=pl.ANY)
 
 
-def params(mebibytes):
-    return pltpu.CompilerParams(vmem_limit_bytes=mebibytes << 20)
+def params(kibibytes=65024):
+    return pltpu.CompilerParams(vmem_limit_bytes=kibibytes << 10)
 
 
 def dot(left, right):
@@ -115,7 +115,7 @@
             pltpu.VMEM(inputs.shape, BF16),
             pltpu.SemaphoreType.DMA((3,)),
         ],
-        compiler_params=params(63),
+        compiler_params=params(),
     )(step_count, emit_steps, initial, conductivity, inputs)
 
 
@@ -197,14 +197,14 @@
             pltpu.SemaphoreType.DMA((pieces,)),
             pltpu.SemaphoreType.DMA((pieces,)),
         ],
-        compiler_params=params(63),
+        compiler_params=params(),
         cost_estimate=pl.CostEstimate(
             flops=0, bytes_accessed=4 * units * rows * cols, transcendentals=0
         ),
     )(weight)
 
 
-def forward(seed_ref, first_ref, second_ref, third_ref, inputs, act_a, act_b, hidden, gate, raw, scratch):
+def forward(seed_ref, first_ref, second_ref, third_ref, inputs, act_a, act_b, hidden, gate, raw):
     devices = seed_ref.shape[0]
     here = inputs.shape[0] // devices
     for d in range(devices):
@@ -216,15 +216,14 @@
     act_b[...] = act
     act = jnp.tanh(dot(act.astype(BF16), third_ref[...]))
     hidden[...] = act.astype(BF16)
-    scratch[...] = 1.0 - act * act
-    fold_rows(scratch, gate)
+    gate[...] = 1.0 - act * act
 
 
 def main_kernel(
     scale, snaps, own_far, top_far, bottom_far, seed_far, low_far, high_far, assign_far, first_far, second_far, third_far,
-    res_far, back_ref, in_far, a_far, b_far, hid_far, gate_far,
+    res_far, back_ref, in_far, a_far, b_far, hid_far,
     state, rate, history, picked, predicted, by_rows, total, raw, assigned, first, second, third,
-    own_ref, top_ref, bottom_ref, seed_ref, res, inputs, act_a, act_b, hidden, gate, arrived, filled, left,
+    own_ref, top_ref, bottom_ref, seed_ref, gather, gate, res, inputs, act_a, act_b, hidden, arrived, filled, left,
 ):
     fields, _, rows, width = own_ref.shape
     _, batch, cols = predicted.shape
@@ -233,8 +232,8 @@
     entries = fields * STEPS
     pitch = entries + 1
     pairs = (
-        (seed_far, seed_ref), (first_far, first), (second_far, second), (third_far, third),
-        (top_far, top_ref), (own_far, own_ref), (bottom_far, bottom_ref), (assign_far, assigned),
+        (top_far, top_ref), (own_far, own_ref), (bottom_far, bottom_ref),
+        (seed_far, seed_ref), (first_far, first), (second_far, second), (third_far, third), (assign_far, assigned),
     )
     loads = [
         pltpu.make_async_copy(source, target, arrived.at[i])
@@ -245,34 +244,25 @@
     together = 2 if fields % 2 == 0 else 1
     parts = STEPS // 8
     turns = fields // together * parts
-    each = -(-rows // (4 * turns))
     fills = [
         [
             pltpu.make_async_copy(
-                source.at[low : low + 4 * each],
-                by_rows.at[low : low + 4 * each, half * units // 2 : (half + 1) * units // 2, :],
-                filled.at[half, low // (4 * each)],
+                source.at[low : low + 4],
+                by_rows.at[low : low + 4, half * units // 2 : (half + 1) * units // 2, :],
+                filled.at[half, low // 4],
             )
             for half, source in enumerate((low_far, high_far))
         ]
-        for low in range(0, rows, 4 * each)
-    ]
+        for low in range(0, rows, 4)
+    ]
+    place = lax.broadcasted_iota(jnp.int32, (width, cols), 0)
+    column = lax.broadcasted_iota(jnp.int32, (width, cols), 1) + STEPS
+    gather[...] = (tiles * (place % LANES) + place // LANES == column).astype(F32).astype(BF16)
+    for load in loads[:3]:
+        load.wait()
     for pair in fills:
         for fill in pair:
             fill.start()
-    for load in loads[:4]:
-        load.wait()
-    forward(seed_ref, first, second, third, inputs, act_a, act_b, hidden, gate, raw, total)
-    stores = [
-        pltpu.make_async_copy(source, target, left.at[i])
-        for i, (source, target) in enumerate(
-            ((inputs, in_far), (act_a, a_far), (act_b, b_far), (hidden, hid_far), (gate, gate_far))
-        )
-    ]
-    for store in stores:
-        store.start()
-    for load in loads[4:]:
-        load.wait()
 
     for f in range(fields):
         for now in range(2):
@@ -286,23 +276,42 @@
                 rate[f, j, low : low + rows, :] = ref[f, 1, :, lane_tile(j)]
                 if place != 1:
                     state[f, 1, j, low : low + rows, :] = ref[f, 0, :, lane_tile(j)]
-    for turn in range(turns):
-        if turn < len(fills):
-            for fill in fills[turn]:
-                fill.wait()
+    def solve(turn, first_row):
         which = [turn // parts * together + i for i in range(together)]
         part = turn % parts
 
         def two_steps(pair, _):
             for now in range(2):
                 advance(state, rate, history, pitch, part, which, now, 2 * pair + now)
-            if turn * 4 * each < rows:
-                for k in range(each):
-                    r = (turn * 4 + pair - 4 * part) * each + k
-                    predicted[r] = dot(hidden[...], by_rows[r])
+            if first_row is not None:
+                r = first_row + pair - 4 * part
+                predicted[r] = dot(hidden[...], by_rows[r])
             return 0
 
         lax.fori_loop(4 * part, 4 * part + 4, two_steps, 0)
+
+    solve(0, None)
+    for load in loads[3:]:
+        load.wait()
+    forward(seed_ref, first, second, third, inputs, act_a, act_b, hidden, gate, raw)
+    stores = [
+        pltpu.make_async_copy(source, target, left.at[i])
+        for i, (source, target) in enumerate(
+            ((inputs, in_far), (act_a, a_far), (act_b, b_far), (hidden, hid_far))
+        )
+    ]
+    for store in stores:
+        store.start()
+    for turn in range(1, turns):
+        if turn <= len(fills):
+            for fill in fills[turn - 1]:
+                fill.wait()
+        solve(turn, 4 * (turn - 1) if turn <= len(fills) else None)
+    for turn in range(turns, len(fills) + 1):
+        for fill in fills[turn - 1]:
+            fill.wait()
+        for r in range(4 * (turn - 1), 4 * turn):
+            predicted[r] = dot(hidden[...], by_rows[r])
 
     lane = lax.broadcasted_iota(jnp.int32, (snaps, entries), 1)
     steps = []
@@ -313,29 +322,25 @@
     number = lax.broadcasted_iota(jnp.int32, (fields * snaps, batch), 0)
     chosen = (number == assigned[...]).astype(F32).astype(BF16)
     hot = contract_rows(chosen, steps).astype(BF16)
-    place = lax.broadcasted_iota(jnp.int32, (width, cols), 0)
-    column = lax.broadcasted_iota(jnp.int32, (width, cols), 1) + STEPS
-    gather = (tiles * (place % LANES) + place // LANES == column).astype(F32).astype(BF16)
-
     chunk = 8
     for i in range(rows // chunk):
         for k in range(chunk):
             low = (i * chunk + k) * pitch
             for j in range(tiles):
                 states = history[j, low : low + entries, :].astype(BF16)
-                picked[k * batch : (k + 1) * batch, lane_tile(j)] = dot(hot, states).astype(BF16)
-        targets = dot(picked[...], gather)
-        back = None
+                picked[i % 2, k * batch : (k + 1) * batch, lane_tile(j)] = dot(hot, states).astype(BF16)
+        targets = dot(picked[i % 2], gather[...])
         for k in range(chunk):
             r = i * chunk + k
             residual = ((predicted[r] - targets[k * batch : (k + 1) * batch]) * scale).astype(BF16)
             res[r] = residual
             part = contract_cols(residual, by_rows[r])
-            back = part if back is None else back + part
+            back = part if k == 0 else back + part
         total[...] = back if i == 0 else total[...] + back
         place = slice(i * chunk, (i + 1) * chunk)
-        stores.append(pltpu.make_async_copy(res.at[place], res_far.at[place], left.at[5 + i]))
+        stores.append(pltpu.make_async_copy(res.at[place], res_far.at[place], left.at[4 + i]))
         stores[-1].start()
+    total[...] = total[...] * gate[...]
     fold_rows(total, back_ref)
     for store in stores:
         store.wait()
@@ -359,19 +364,18 @@
         ((batch, units), F32),
         ((batch, units), F32),
         ((batch, units), BF16),
-        (folded, F32),
     ]
     shapes = [jax.ShapeDtypeStruct(*k) for k in kept]
     return pl.pallas_call(
         functools.partial(main_kernel, scale, snaps),
         in_specs=[far] * 10,
-        out_specs=[far, whole] + [far] * 5,
+        out_specs=[far, whole] + [far] * 4,
         out_shape=[shapes[0], jax.ShapeDtypeStruct(folded, F32)] + shapes[1:],
         scratch_shapes=[
             pltpu.VMEM((fields, 2, tiles, depth, LANES), F32),
             pltpu.VMEM((fields, tiles, depth, LANES), F32),
             pltpu.VMEM((tiles, rows * (entries + 1), LANES), F32),
-            pltpu.VMEM((8 * batch, width), BF16),
+            pltpu.VMEM((2, 8 * batch, width), BF16),
             pltpu.VMEM((rows, batch, cols), F32),
             pltpu.VMEM((rows, units, cols), BF16),
             pltpu.VMEM((batch, units), F32),
@@ -384,14 +388,16 @@
             pltpu.VMEM(own.shape, F32),
             pltpu.VMEM(own.shape, F32),
             pltpu.VMEM(seeds.shape, F32),
+            pltpu.VMEM((width, cols), BF16),
+            pltpu.VMEM((batch, units), F32),
         ]
         + [pltpu.VMEM(*k) for k in kept]
         + [
             pltpu.SemaphoreType.DMA((8,)),
             pltpu.SemaphoreType.DMA((2, rows // 4)),
-            pltpu.SemaphoreType.DMA((5 + rows // 8,)),
+            pltpu.SemaphoreType.DMA((4 + rows // 8,)),
         ],
-        compiler_params=params(63),
+        compiler_params=params(),
     )(own, top, bottom, seeds, *halves, assign.reshape(1, batch), w_first, w_second, w_third)
 
 
@@ -420,7 +426,7 @@
         out_specs=pl.BlockSpec((chunk, rows, cols), lambda i: (i, 0, 0)),
         out_shape=jax.ShapeDtypeStruct((units, rows, cols), BF16),
         scratch_shapes=[pltpu.VMEM((rows, chunk, cols), BF16)],
-        compiler_params=params(63),
+        compiler_params=params(),
         cost_estimate=pl.CostEstimate(
             flops=2 * batch * units * rows * cols,
             bytes_accessed=4 * units * rows * cols,
@@ -429,37 +435,24 @@
     )(hidden, res)
 
 
-def delta_kernel(pieces_far, gate_far, out_ref, pieces, gate, arrived):
+def delta_kernel(pieces, out_ref):
     devices = pieces.shape[0]
-    loads = [
-        pltpu.make_async_copy(pieces_far, pieces, arrived.at[0]),
-        pltpu.make_async_copy(gate_far.at[lax.axis_index(ALL)], gate, arrived.at[1]),
-    ]
-    for load in loads:
-        load.start()
-    for load in loads:
-        load.wait()
-    back = [pieces[d] for d in range(devices)]
-    while len(back) > 1:
-        back = [a + b for a, b in zip(back[::2], back[1::2])] + back[len(back) // 2 * 2 :]
-    delta = (back[0] * gate[...]).astype(BF16)
+    delta = [pieces[d] for d in range(devices)]
+    while len(delta) > 1:
+        delta = [a + b for a, b in zip(delta[::2], delta[1::2])] + delta[len(delta) // 2 * 2 :]
+    delta = delta[0].astype(BF16)
     for d in range(devices):
         out_ref[d] = delta
 
 
-def delta_spread(pieces, gate):
+def delta_spread(pieces):
     return pl.pallas_call(
         delta_kernel,
-        in_specs=[far, far],
+        in_specs=[whole],
         out_specs=whole,
         out_shape=jax.ShapeDtypeStruct(pieces.shape, BF16),
-        scratch_shapes=[
-            pltpu.VMEM(pieces.shape, F32),
-            pltpu.VMEM(gate.shape[1:], F32),
-            pltpu.SemaphoreType.DMA((2,)),
-        ],
-        compiler_params=params(63),
-    )(pieces, gate)
+        compiler_params=params(16384),
+    )(pieces)
 
 
 def backward_kernel(
@@ -530,7 +523,7 @@
         ]
         + [pltpu.VMEM(shape, F32) for shape in shapes]
         + [pltpu.SemaphoreType.DMA((6,)), pltpu.SemaphoreType.DMA((3,))],
-        compiler_params=params(63),
+        compiler_params=params(),
     )(inputs, act_a, act_b, delta, w_second, w_third)
 
 
@@ -566,14 +559,14 @@
     bottom = lax.ppermute(own, "strip", [(j, i) for i, j in down])
     own, seeds = lax.optimization_barrier((own, seeds))
     seeds = swap(seeds, ALL)
-    res, partial, inputs, act_a, act_b, hidden, gate = main(
+    res, partial, inputs, act_a, act_b, hidden = main(
         assign, own, top, bottom, seeds, w_first, w_second, w_third, (low, by_row(w_out, 1)),
         emit_steps.shape[1], here, fold,
     )
     pieces = swap(partial, ALL)
     grad_out = outer(hidden, res)
     pieces, grad_out = lax.optimization_barrier((pieces, grad_out))
-    delta = swap(delta_spread(pieces, gate), ALL)
+    delta = swap(delta_spread(pieces), ALL)
     grads = backward(inputs, act_a, act_b, delta, w_second, w_third)
     return (*grads, grad_out)
 

time: 83.4 us -> 78.9 us (0.946)
  Pallas kernels: 41.5 us -> 37.9 us
  local copies, waits for them, and re-layouts: 1.48 us -> 0.01 us
    pallas_call x1, Pallas kernels: 18.2 us -> 16.3 us  [main(): pl.pallas_call(functools.partial(main_kernel, scale, snaps), in_specs=[fa...]
    pallas_call x1, Pallas kernels: 1.65 us -> 0.03 us  [delta_spread(): pl.pallas_call(delta_kernel, in_specs=[whole], out_specs=whole, out_shape...]
    unnamed x8 -> x2, local copies, waits for them, and re-layouts: 1.48 us -> 0.01 us
    all_to_all x3, starting transfers between devices: 11.9 us -> 12.8 us  [swap(): return lax.all_to_all(value, axes, split_axis=0, concat_axis=0, tiled=True)]
  transfers between devices with their start and end apart: 5 -> 5, of which waited for: 3 -> 3; matrix products, arithmetic and copies ran while one was open for 0% -> 0% of each run, Pallas kernels for 19% -> 20%
where the time goes in v4:
time: 78.9 us; the launch traced here: 78.4 us
  Pallas kernels  37.9 us (48%)
  starting transfers between devices  17.8 us (23%)
  blocking collectives  11.6 us (15%)
  waiting for transfers between devices  9.71 us (12%)
  between operations  1.35 us (2%)
    pallas_call x1, Pallas kernels, main(): pl.pallas_call(functools.partial(main_kernel, scale, snaps), in_specs=[fa...  16.3 us
    all_to_all x3, starting transfers between devices, swap(): return lax.all_to_all(value, axes, split_axis=0, concat_axis=0, tiled=True)  12.8 us
    all_to_all x1, blocking collectives, swap(): return lax.all_to_all(value, axes, split_axis=0, concat_axis=0, tiled=True)  11.6 us
    all_to_all x3, waiting for transfers between devices, swap(): return lax.all_to_all(value, axes, split_axis=0, concat_axis=0, tiled=True)  9.71 us
    pallas_call x1, Pallas kernels, outer(): pl.pallas_call(outer_kernel, grid=(units // chunk,), in_specs=[pl.BlockSp...  8.05 us
    pallas_call x2, Pallas kernels, by_row(): pl.pallas_call(functools.partial(by_row_kernel, half * units), in_specs=[...  7.36 us
    ppermute x1, starting transfers between devices, per_device(): top = lax.ppermute(own, 'strip', down)  3.8 us
    pallas_call x1, Pallas kernels, backward(): pl.pallas_call(backward_kernel, in_specs=[far] * 6, out_specs=[far] * 3,...  3.26 us
  transfers between devices with their start and end apart: 5, of which 3 were waited for; matrix products, arithmetic and copies ran while one was open for 0% of the time, Pallas kernels for 20%

profile of v4, /device:TPU:0, one launch (start us, length us, event | category | flops | bytes accessed | tf_op | source)
XLA Modules:
  0.0 78.4 jit_solution(2593761393043733941)
XLA Ops:
  1.3 3.0 %shard_map.129 = (f32[4,2,32,384]{3,2,1,0:T(8,128)}, f32[32,8,128]{2,1,0:T(8,128)}) custom-call(s32[1]{0:T(128)S(6)} %copy.14.count_ref, s32[1,16]{1,0:T(1,128)} %emit_ref.1, f32[1,32,1024]{2,1,0:T(8,128)} %field_far.1, f32[1,32,1024]{2,1,0:T(8,128)} %kappa_far.1, bf16[4,128]{1,0:T(4,128)(2,1)} %inputs_far.1), custom_call_target="tpu_custom_call" | custom-call | tf_op jit(solution)/shard_map/pallas_call | solution.py:104
  4.3 5.2 %all-to-all-start = ((f32[4,2,32,384]{3,2,1,0:T(8,128)}), f32[4,2,32,384]{3,2,1,0:T(8,128)S(1)}, u32[]{:S(2)}, u32[]{:S(2)}) async-start(f32[4,2,32,384]{3,2,1,0:T(8,128)} %get-tuple-element.25), calls=%async_computation | async-start | bytes 786432 | tf_op jit(solution)/shard_map/all_to_all | solution.py:531
  9.4 3.7 %shard_map.130.low_far = bf16[32,256,256]{2,1,0:T(8,128)(2,1)} custom-call(bf16[512,32,256]{2,1,0:T(8,128)(2,1)} %weight_far.1), custom_call_target="tpu_custom_call" | custom-call | bytes 8388608 | tf_op jit(solution)/shard_map/pallas_call | solution.py:189
  13.1 3.0 %all-to-all-done.own_far = f32[4,2,32,384]{3,2,1,0:T(8,128)S(1)} async-done(((f32[4,2,32,384]{3,2,1,0:T(8,128)}), f32[4,2,32,384]{3,2,1,0:T(8,128)S(1)}, u32[]{:S(2)}, u32[]{:S(2)}) %all-to-all-start) | async-done | bytes 393248 | tf_op jit(solution)/shard_map/all_to_all | solution.py:531
  16.0 0.0 copy-start
  16.1 1.3 %collective-permute-start.1 = (f32[4,2,32,384]{3,2,1,0:T(8,128)S(1)}, f32[4,2,32,384]{3,2,1,0:T(8,128)}, u32[]{:S(2)}, u32[]{:S(2)}) collective-permute-start(f32[4,2,32,384]{3,2,1,0:T(8,128)S(1)} %all-to-all-done.own_far), channel_id=1, source_target_pairs={{1,0},{2,1},{3,2},{4,3},{5,4},{6,5},{7,6},{9,8},{10,9},{11,10},{12... | collective-permute-start | bytes 1179656 | tf_op jit(solution)/shard_map/ppermute | solution.py:559
  17.3 3.8 %collective-permute-start = (f32[4,2,32,384]{3,2,1,0:T(8,128)S(1)}, f32[4,2,32,384]{3,2,1,0:T(8,128)}, u32[]{:S(2)}, u32[]{:S(2)}) collective-permute-start(f32[4,2,32,384]{3,2,1,0:T(8,128)S(1)} %all-to-all-done.own_far), channel_id=1, source_target_pairs={{0,1},{1,2},{2,3},{3,4},{4,5},{5,6},{6,7},{8,9},{9,10},{10,11},{11... | collective-permute-start | bytes 1179656 | tf_op jit(solution)/shard_map/ppermute | solution.py:558
  21.1 5.0 %all-to-all-start.1 = ((f32[32,8,128]{2,1,0:T(8,128)}), f32[32,8,128]{2,1,0:T(8,128)}, u32[]{:S(2)}, u32[]{:S(2)}) async-start(f32[32,8,128]{2,1,0:T(8,128)} %get-tuple-element.30), calls=%async_computation.1 | async-start | bytes 262144 | tf_op jit(solution)/shard_map/all_to_all | solution.py:531
  26.1 3.7 %shard_map.131.high_far = bf16[32,256,256]{2,1,0:T(8,128)(2,1)} custom-call(bf16[512,32,256]{2,1,0:T(8,128)(2,1)} %weight_far.1), custom_call_target="tpu_custom_call" | custom-call | bytes 8388608 | tf_op jit(solution)/shard_map/pallas_call | solution.py:189
  29.9 0.0 copy-done
  29.9 4.4 %all-to-all-done.1.seed_far = f32[32,8,128]{2,1,0:T(8,128)} async-done(((f32[32,8,128]{2,1,0:T(8,128)}), f32[32,8,128]{2,1,0:T(8,128)}, u32[]{:S(2)}, u32[]{:S(2)}) %all-to-all-start.1) | async-done | bytes 131104 | tf_op jit(solution)/shard_map/all_to_all | solution.py:531
  34.3 0.0 collective-permute-done.1.bottom_far
  34.3 0.0 collective-permute-done.top_far
  34.3 16.3 %shard_map.132 = (bf16[32,128,256]{2,1,0:T(8,128)(2,1)}, f32[32,8,256]{2,1,0:T(8,128)}, bf16[128,128]{1,0:T(8,128)(2,1)}, f32[128,512]{1,0:T(8,128)}, f32[128,512]{1,0:T(8,128)}, /*index=5*/bf16[128,512]{1,0:T(8,128)(2,1)}) custom-call(f32[4,2,32,384]{3,2,1,0:T(8,128)} %copy-done, f32[4,2,32,384]{3,2,1,0:T(8,128)} %collective-permute-done.top_far, ...), custom_call_target="tpu_custom_call" | custom-call | tf_op jit(solution)/shard_map/pallas_call | solution.py:369
  50.6 2.6 %all-to-all-start.2 = ((f32[32,8,256]{2,1,0:T(8,128)}), f32[32,8,256]{2,1,0:T(8,128)S(1)}, u32[]{:S(2)}, u32[]{:S(2)}) async-start(f32[32,8,256]{2,1,0:T(8,128)} %get-tuple-element.36), calls=%async_computation.2 | async-start | bytes 524288 | tf_op jit(solution)/shard_map/all_to_all | solution.py:531
  53.2 8.0 %shard_map.133 = bf16[512,32,256]{2,1,0:T(8,128)(2,1)} custom-call(bf16[128,512]{1,0:T(8,128)(2,1)} %get-tuple-element.37.hid_ref, bf16[32,128,256]{2,1,0:T(8,128)(2,1)} %get-tuple-element.38.res_ref), custom_call_target="tpu_custom_call" | custom-call | flops 1073741824 | bytes 16777216 | tf_op jit(solution)/shard_map/pallas_call | solution.py:419
  61.2 2.3 %all-to-all-done.2.pieces = f32[32,8,256]{2,1,0:T(8,128)S(1)} async-done(((f32[32,8,256]{2,1,0:T(8,128)}), f32[32,8,256]{2,1,0:T(8,128)S(1)}, u32[]{:S(2)}, u32[]{:S(2)}) %all-to-all-start.2) | async-done | bytes 262176 | tf_op jit(solution)/shard_map/all_to_all | solution.py:531
  63.6 11.6 %all_to_all.20.delta_far = bf16[32,8,256]{2,1,0:T(8,128)(2,1)} all-to-all(bf16[32,8,256]{2,1,0:T(8,128)(2,1)S(1)} %shard_map.134), channel_id=1, replica_groups=mesh['group'=4,'strip'=8] {'group','strip'}, dimensions={0} | all-to-all | bytes 262144 | tf_op jit(solution)/shard_map/all_to_all | solution.py:531
  75.2 3.3 %shard_map.135 = (f32[128,512]{1,0:T(8,128)}, f32[512,512]{1,0:T(8,128)}, f32[512,512]{1,0:T(8,128)}) custom-call(bf16[128,128]{1,0:T(8,128)(2,1)} %get-tuple-element.33.inputs_far, f32[128,512]{1,0:T(8,128)} %get-tuple-element.34.a_far, f32[128,512]{1,0:T(8,128)} %get-tuple-element.35.b_far, bf16[32,8,256]{2,1,0:T(8,128)(2,1)} %all_to_all.20.delta_far, ...), custom_call_target="tpu_custom_call" | custom-call | tf_op jit(solution)/shard_map/pallas_call | solution.py:509
  (1 shorter events, 0.0 us)
Async XLA Ops:
  4.3 11.8 %all-to-all-start = ((f32[4,2,32,384]{3,2,1,0:T(8,128)}), f32[4,2,32,384]{3,2,1,0:T(8,128)S(1)}, u32[]{:S(2)}, u32[]{:S(2)}) async-start(f32[4,2,32,384]{3,2,1,0:T(8,128)} %get-tuple-element.25), calls=%async_computation | async-start | bytes 786432 | tf_op jit(solution)/shard_map/all_to_all | solution.py:531
  16.0 13.8 %copy-start = (f32[4,2,32,384]{3,2,1,0:T(8,128)}, f32[4,2,32,384]{3,2,1,0:T(8,128)S(1)}, u32[]{:S(2)}) copy-start(f32[4,2,32,384]{3,2,1,0:T(8,128)S(1)} %all-to-all-done.own_far) | copy-start | bytes 1179652
  16.1 18.2 %collective-permute-start.1 = (f32[4,2,32,384]{3,2,1,0:T(8,128)S(1)}, f32[4,2,32,384]{3,2,1,0:T(8,128)}, u32[]{:S(2)}, u32[]{:S(2)}) collective-permute-start(f32[4,2,32,384]{3,2,1,0:T(8,128)S(1)} %all-to-all-done.own_far), channel_id=1, source_target_pairs={{1,0},{2,1},{3,2},{4,3},{5,4},{6,5},{7,6},{9,8},{10,9},{11,10},{12... | collective-permute-start | bytes 1179656 | tf_op jit(solution)/shard_map/ppermute | solution.py:559
  17.3 17.0 %collective-permute-start = (f32[4,2,32,384]{3,2,1,0:T(8,128)S(1)}, f32[4,2,32,384]{3,2,1,0:T(8,128)}, u32[]{:S(2)}, u32[]{:S(2)}) collective-permute-start(f32[4,2,32,384]{3,2,1,0:T(8,128)S(1)} %all-to-all-done.own_far), channel_id=1, source_target_pairs={{0,1},{1,2},{2,3},{3,4},{4,5},{5,6},{6,7},{8,9},{9,10},{10,11},{11... | collective-permute-start | bytes 1179656 | tf_op jit(solution)/shard_map/ppermute | solution.py:558
  21.1 13.1 %all-to-all-start.1 = ((f32[32,8,128]{2,1,0:T(8,128)}), f32[32,8,128]{2,1,0:T(8,128)}, u32[]{:S(2)}, u32[]{:S(2)}) async-start(f32[32,8,128]{2,1,0:T(8,128)} %get-tuple-element.30), calls=%async_computation.1 | async-start | bytes 262144 | tf_op jit(solution)/shard_map/all_to_all | solution.py:531
  50.6 13.0 %all-to-all-start.2 = ((f32[32,8,256]{2,1,0:T(8,128)}), f32[32,8,256]{2,1,0:T(8,128)S(1)}, u32[]{:S(2)}, u32[]{:S(2)}) async-start(f32[32,8,256]{2,1,0:T(8,128)} %get-tuple-element.36), calls=%async_computation.2 | async-start | bytes 524288 | tf_op jit(solution)/shard_map/all_to_all | solution.py:531

commit v5 on v4

--- a/solution.py
+++ b/solution.py
@@ -45,7 +45,8 @@
 
 
 def split_kernel(
-    count_ref, emit_ref, field_far, kappa_far, inputs_far, out_ref, seed_ref, field_ref, kappa_ref, inputs_ref, arrived
+    count_ref, emit_ref, field_far, kappa_far, inputs_far, out_far, seed_far,
+    field_ref, kappa_ref, inputs_ref, out_ref, seed_ref, arrived, left,
 ):
     loads = [
         pltpu.make_async_copy(source, target, arrived.at[i])
@@ -64,7 +65,17 @@
     place = lax.broadcasted_iota(jnp.int32, (span, width), 1)
     wanted = tiles * (place % LANES) + place // LANES
     deal = ((source == wanted) & (wanted < cols + 2 * STEPS)).astype(F32).astype(BF16)
-    for load in loads:
+    stores = [pltpu.make_async_copy(seed_ref, seed_far, left.at[blocks])]
+    loads[2].wait()
+    here = inputs_ref.shape[0]
+    devices, deep, features = seed_ref.shape
+    seed = inputs_ref[...].astype(F32)
+    if deep > here:
+        seed = jnp.concatenate([seed, jnp.zeros((deep - here, features), F32)], axis=0)
+    for d in range(devices):
+        seed_ref[d] = seed
+    stores[0].start()
+    for load in loads[:2]:
         load.wait()
     none = jnp.zeros((2 * rows, LANES), F32)
     both = jnp.concatenate([field_ref[0], kappa_ref[0] * step_rate], axis=0)
@@ -88,13 +99,10 @@
         out_ref[g, 0] = dealt[:rows]
         out_ref[g, 1] = dealt[rows:]
         out_ref[g, 0, :, :LANES] = jnp.where(lane == META, meta, dealt[:rows, :LANES])
-    here = inputs_ref.shape[0]
-    devices, deep, features = seed_ref.shape
-    seed = inputs_ref[...].astype(F32)
-    if deep > here:
-        seed = jnp.concatenate([seed, jnp.zeros((deep - here, features), F32)], axis=0)
-    for d in range(devices):
-        seed_ref[d] = seed
+        stores.append(pltpu.make_async_copy(out_ref.at[g], out_far.at[g], left.at[g]))
+        stores[-1].start()
+    for store in stores:
+        store.wait()
 
 
 def split_columns(initial, conductivity, step_count, emit_steps, inputs, blocks, devices):
@@ -104,7 +112,7 @@
     return pl.pallas_call(
         split_kernel,
         in_specs=[scalars, scalars, far, far, far],
-        out_specs=[whole, whole],
+        out_specs=[far, far],
         out_shape=[
             jax.ShapeDtypeStruct((blocks, 2, rows, width), F32),
             jax.ShapeDtypeStruct((devices, -(-here // 8) * 8, features), F32),
@@ -113,7 +121,10 @@
             pltpu.VMEM(initial.shape, F32),
             pltpu.VMEM(conductivity.shape, F32),
             pltpu.VMEM(inputs.shape, BF16),
+            pltpu.VMEM((blocks, 2, rows, width), F32),
+            pltpu.VMEM((devices, -(-here // 8) * 8, features), F32),
             pltpu.SemaphoreType.DMA((3,)),
+            pltpu.SemaphoreType.DMA((blocks + 1,)),
         ],
         compiler_params=params(),
     )(step_count, emit_steps, initial, conductivity, inputs)
@@ -290,10 +301,14 @@
 
         lax.fori_loop(4 * part, 4 * part + 4, two_steps, 0)
 
-    solve(0, None)
+    which = list(range(together))
+    for t in range(4):
+        advance(state, rate, history, pitch, 0, which, t % 2, t)
     for load in loads[3:]:
         load.wait()
     forward(seed_ref, first, second, third, inputs, act_a, act_b, hidden, gate, raw)
+    for t in range(4, 8):
+        advance(state, rate, history, pitch, 0, which, t % 2, t)
     stores = [
         pltpu.make_async_copy(source, target, left.at[i])
         for i, (source, target) in enumerate(

time: 78.9 us -> 78.5 us (level)
  no operation moved by 1% of the time
where the time goes in v5:
time: 78.5 us; the launch traced here: 78 us
  Pallas kernels  37.5 us (48%)
  starting transfers between devices  17.8 us (23%)
  blocking collectives  11.6 us (15%)
  waiting for transfers between devices  9.71 us (12%)
  between operations  1.35 us (2%)
    pallas_call x1, Pallas kernels, main(): pl.pallas_call(functools.partial(main_kernel, scale, snaps), in_specs=[fa...  15.9 us
    all_to_all x3, starting transfers between devices, swap(): return lax.all_to_all(value, axes, split_axis=0, concat_axis=0, tiled=True)  12.8 us
    all_to_all x1, blocking collectives, swap(): return lax.all_to_all(value, axes, split_axis=0, concat_axis=0, tiled=True)  11.6 us
    all_to_all x3, waiting for transfers between devices, swap(): return lax.all_to_all(value, axes, split_axis=0, concat_axis=0, tiled=True)  9.71 us
    pallas_call x1, Pallas kernels, outer(): pl.pallas_call(outer_kernel, grid=(units // chunk,), in_specs=[pl.BlockSp...  8.05 us
    pallas_call x2, Pallas kernels, by_row(): pl.pallas_call(functools.partial(by_row_kernel, half * units), in_specs=[...  7.36 us
    ppermute x1, starting transfers between devices, per_device(): top = lax.ppermute(own, 'strip', down)  3.8 us
    pallas_call x1, Pallas kernels, backward(): pl.pallas_call(backward_kernel, in_specs=[far] * 6, out_specs=[far] * 3,...  3.26 us
  transfers between devices with their start and end apart: 5, of which 3 were waited for; matrix products, arithmetic and copies ran while one was open for 0% of the time, Pallas kernels for 20%

profile of v5, /device:TPU:0, one launch (start us, length us, event | category | flops | bytes accessed | tf_op | source)
XLA Modules:
  0.0 78.0 jit_solution(7784511781140685075)
XLA Ops:
  1.3 2.9 %shard_map.129 = (f32[4,2,32,384]{3,2,1,0:T(8,128)}, f32[32,8,128]{2,1,0:T(8,128)}) custom-call(s32[1]{0:T(128)S(6)} %copy.14.count_ref, s32[1,16]{1,0:T(1,128)} %emit_ref.1, f32[1,32,1024]{2,1,0:T(8,128)} %field_far.1, f32[1,32,1024]{2,1,0:T(8,128)} %kappa_far.1, bf16[4,128]{1,0:T(4,128)(2,1)} %inputs_far.1), custom_call_target="tpu_custom_call" | custom-call | tf_op jit(solution)/shard_map/pallas_call | solution.py:112
  4.2 5.2 %all-to-all-start = ((f32[4,2,32,384]{3,2,1,0:T(8,128)}), f32[4,2,32,384]{3,2,1,0:T(8,128)S(1)}, u32[]{:S(2)}, u32[]{:S(2)}) async-start(f32[4,2,32,384]{3,2,1,0:T(8,128)} %get-tuple-element.25), calls=%async_computation | async-start | bytes 786432 | tf_op jit(solution)/shard_map/all_to_all | solution.py:546
  9.4 3.7 %shard_map.130.low_far = bf16[32,256,256]{2,1,0:T(8,128)(2,1)} custom-call(bf16[512,32,256]{2,1,0:T(8,128)(2,1)} %weight_far.1), custom_call_target="tpu_custom_call" | custom-call | bytes 8388608 | tf_op jit(solution)/shard_map/pallas_call | solution.py:200
  13.0 3.0 %all-to-all-done.own_far = f32[4,2,32,384]{3,2,1,0:T(8,128)S(1)} async-done(((f32[4,2,32,384]{3,2,1,0:T(8,128)}), f32[4,2,32,384]{3,2,1,0:T(8,128)S(1)}, u32[]{:S(2)}, u32[]{:S(2)}) %all-to-all-start) | async-done | bytes 393248 | tf_op jit(solution)/shard_map/all_to_all | solution.py:546
  16.0 0.0 copy-start
  16.0 1.3 %collective-permute-start.1 = (f32[4,2,32,384]{3,2,1,0:T(8,128)S(1)}, f32[4,2,32,384]{3,2,1,0:T(8,128)}, u32[]{:S(2)}, u32[]{:S(2)}) collective-permute-start(f32[4,2,32,384]{3,2,1,0:T(8,128)S(1)} %all-to-all-done.own_far), channel_id=1, source_target_pairs={{1,0},{2,1},{3,2},{4,3},{5,4},{6,5},{7,6},{9,8},{10,9},{11,10},{12... | collective-permute-start | bytes 1179656 | tf_op jit(solution)/shard_map/ppermute | solution.py:574
  17.3 3.8 %collective-permute-start = (f32[4,2,32,384]{3,2,1,0:T(8,128)S(1)}, f32[4,2,32,384]{3,2,1,0:T(8,128)}, u32[]{:S(2)}, u32[]{:S(2)}) collective-permute-start(f32[4,2,32,384]{3,2,1,0:T(8,128)S(1)} %all-to-all-done.own_far), channel_id=1, source_target_pairs={{0,1},{1,2},{2,3},{3,4},{4,5},{5,6},{6,7},{8,9},{9,10},{10,11},{11... | collective-permute-start | bytes 1179656 | tf_op jit(solution)/shard_map/ppermute | solution.py:573
  21.1 5.0 %all-to-all-start.1 = ((f32[32,8,128]{2,1,0:T(8,128)}), f32[32,8,128]{2,1,0:T(8,128)}, u32[]{:S(2)}, u32[]{:S(2)}) async-start(f32[32,8,128]{2,1,0:T(8,128)} %get-tuple-element.30), calls=%async_computation.1 | async-start | bytes 262144 | tf_op jit(solution)/shard_map/all_to_all | solution.py:546
  26.1 3.7 %shard_map.131.high_far = bf16[32,256,256]{2,1,0:T(8,128)(2,1)} custom-call(bf16[512,32,256]{2,1,0:T(8,128)(2,1)} %weight_far.1), custom_call_target="tpu_custom_call" | custom-call | bytes 8388608 | tf_op jit(solution)/shard_map/pallas_call | solution.py:200
  29.8 0.0 copy-done
  29.8 4.4 %all-to-all-done.1.seed_far = f32[32,8,128]{2,1,0:T(8,128)} async-done(((f32[32,8,128]{2,1,0:T(8,128)}), f32[32,8,128]{2,1,0:T(8,128)}, u32[]{:S(2)}, u32[]{:S(2)}) %all-to-all-start.1) | async-done | bytes 131104 | tf_op jit(solution)/shard_map/all_to_all | solution.py:546
  34.2 0.0 collective-permute-done.1.bottom_far
  34.2 0.0 collective-permute-done.top_far
  34.2 15.9 %shard_map.132 = (bf16[32,128,256]{2,1,0:T(8,128)(2,1)}, f32[32,8,256]{2,1,0:T(8,128)}, bf16[128,128]{1,0:T(8,128)(2,1)}, f32[128,512]{1,0:T(8,128)}, f32[128,512]{1,0:T(8,128)}, /*index=5*/bf16[128,512]{1,0:T(8,128)(2,1)}) custom-call(f32[4,2,32,384]{3,2,1,0:T(8,128)} %copy-done, f32[4,2,32,384]{3,2,1,0:T(8,128)} %collective-permute-done.top_far, ...), custom_call_target="tpu_custom_call" | custom-call | tf_op jit(solution)/shard_map/pallas_call | solution.py:384
  50.2 2.6 %all-to-all-start.2 = ((f32[32,8,256]{2,1,0:T(8,128)}), f32[32,8,256]{2,1,0:T(8,128)S(1)}, u32[]{:S(2)}, u32[]{:S(2)}) async-start(f32[32,8,256]{2,1,0:T(8,128)} %get-tuple-element.36), calls=%async_computation.2 | async-start | bytes 524288 | tf_op jit(solution)/shard_map/all_to_all | solution.py:546
  52.8 8.0 %shard_map.133 = bf16[512,32,256]{2,1,0:T(8,128)(2,1)} custom-call(bf16[128,512]{1,0:T(8,128)(2,1)} %get-tuple-element.37.hid_ref, bf16[32,128,256]{2,1,0:T(8,128)(2,1)} %get-tuple-element.38.res_ref), custom_call_target="tpu_custom_call" | custom-call | flops 1073741824 | bytes 16777216 | tf_op jit(solution)/shard_map/pallas_call | solution.py:434
  60.8 2.3 %all-to-all-done.2.pieces = f32[32,8,256]{2,1,0:T(8,128)S(1)} async-done(((f32[32,8,256]{2,1,0:T(8,128)}), f32[32,8,256]{2,1,0:T(8,128)S(1)}, u32[]{:S(2)}, u32[]{:S(2)}) %all-to-all-start.2) | async-done | bytes 262176 | tf_op jit(solution)/shard_map/all_to_all | solution.py:546
  63.2 11.6 %all_to_all.20.delta_far = bf16[32,8,256]{2,1,0:T(8,128)(2,1)} all-to-all(bf16[32,8,256]{2,1,0:T(8,128)(2,1)S(1)} %shard_map.134), channel_id=1, replica_groups=mesh['group'=4,'strip'=8] {'group','strip'}, dimensions={0} | all-to-all | bytes 262144 | tf_op jit(solution)/shard_map/all_to_all | solution.py:546
  74.8 3.3 %shard_map.135 = (f32[128,512]{1,0:T(8,128)}, f32[512,512]{1,0:T(8,128)}, f32[512,512]{1,0:T(8,128)}) custom-call(bf16[128,128]{1,0:T(8,128)(2,1)} %get-tuple-element.33.inputs_far, f32[128,512]{1,0:T(8,128)} %get-tuple-element.34.a_far, f32[128,512]{1,0:T(8,128)} %get-tuple-element.35.b_far, bf16[32,8,256]{2,1,0:T(8,128)(2,1)} %all_to_all.20.delta_far, ...), custom_call_target="tpu_custom_call" | custom-call | tf_op jit(solution)/shard_map/pallas_call | solution.py:524
  (1 shorter events, 0.0 us)
Async XLA Ops:
  4.2 11.8 %all-to-all-start = ((f32[4,2,32,384]{3,2,1,0:T(8,128)}), f32[4,2,32,384]{3,2,1,0:T(8,128)S(1)}, u32[]{:S(2)}, u32[]{:S(2)}) async-start(f32[4,2,32,384]{3,2,1,0:T(8,128)} %get-tuple-element.25), calls=%async_computation | async-start | bytes 786432 | tf_op jit(solution)/shard_map/all_to_all | solution.py:546
  16.0 13.8 %copy-start = (f32[4,2,32,384]{3,2,1,0:T(8,128)}, f32[4,2,32,384]{3,2,1,0:T(8,128)S(1)}, u32[]{:S(2)}) copy-start(f32[4,2,32,384]{3,2,1,0:T(8,128)S(1)} %all-to-all-done.own_far) | copy-start | bytes 1179652
  16.0 18.2 %collective-permute-start.1 = (f32[4,2,32,384]{3,2,1,0:T(8,128)S(1)}, f32[4,2,32,384]{3,2,1,0:T(8,128)}, u32[]{:S(2)}, u32[]{:S(2)}) collective-permute-start(f32[4,2,32,384]{3,2,1,0:T(8,128)S(1)} %all-to-all-done.own_far), channel_id=1, source_target_pairs={{1,0},{2,1},{3,2},{4,3},{5,4},{6,5},{7,6},{9,8},{10,9},{11,10},{12... | collective-permute-start | bytes 1179656 | tf_op jit(solution)/shard_map/ppermute | solution.py:574
  17.3 17.0 %collective-permute-start = (f32[4,2,32,384]{3,2,1,0:T(8,128)S(1)}, f32[4,2,32,384]{3,2,1,0:T(8,128)}, u32[]{:S(2)}, u32[]{:S(2)}) collective-permute-start(f32[4,2,32,384]{3,2,1,0:T(8,128)S(1)} %all-to-all-done.own_far), channel_id=1, source_target_pairs={{0,1},{1,2},{2,3},{3,4},{4,5},{5,6},{6,7},{8,9},{9,10},{10,11},{11... | collective-permute-start | bytes 1179656 | tf_op jit(solution)/shard_map/ppermute | solution.py:573
  21.1 13.1 %all-to-all-start.1 = ((f32[32,8,128]{2,1,0:T(8,128)}), f32[32,8,128]{2,1,0:T(8,128)}, u32[]{:S(2)}, u32[]{:S(2)}) async-start(f32[32,8,128]{2,1,0:T(8,128)} %get-tuple-element.30), calls=%async_computation.1 | async-start | bytes 262144 | tf_op jit(solution)/shard_map/all_to_all | solution.py:546
  50.2 13.0 %all-to-all-start.2 = ((f32[32,8,256]{2,1,0:T(8,128)}), f32[32,8,256]{2,1,0:T(8,128)S(1)}, u32[]{:S(2)}, u32[]{:S(2)}) async-start(f32[32,8,256]{2,1,0:T(8,128)} %get-tuple-element.36), calls=%async_computation.2 | async-start | bytes 524288 | tf_op jit(solution)/shard_map/all_to_all | solution.py:546

commit v6 on v5

--- a/solution.py
+++ b/solution.py
@@ -389,7 +389,7 @@
         scratch_shapes=[
             pltpu.VMEM((fields, 2, tiles, depth, LANES), F32),
             pltpu.VMEM((fields, tiles, depth, LANES), F32),
-            pltpu.VMEM((tiles, rows * (entries + 1), LANES), F32),
+            pltpu.VMEM((tiles, (rows + 1) * (entries + 1), LANES), F32),
             pltpu.VMEM((2, 8 * batch, width), BF16),
             pltpu.VMEM((rows, batch, cols), F32),
             pltpu.VMEM((rows, units, cols), BF16),
@@ -561,7 +561,7 @@
     groups, strips = lax.axis_size("group"), lax.axis_size("strip")
     devices = groups * strips
     here = sample_inputs.shape[0]
-    fold = max(1, 8 // here)
+    fold = max(1, 16 // here)
     blocks, seeds = split_columns(
         initial, conductivity, step_count, emit_steps, sample_inputs, groups, devices
     )

time: 78.5 us -> 78.7 us (level)
  no operation moved by 1% of the time
where the time goes in v6:
time: 78.7 us; the launch traced here: 78.2 us
  Pallas kernels  37.7 us (48%)
  starting transfers between devices  17.8 us (23%)
  blocking collectives  11.6 us (15%)
  waiting for transfers between devices  9.71 us (12%)
  between operations  1.35 us (2%)
    pallas_call x1, Pallas kernels, main(): pl.pallas_call(functools.partial(main_kernel, scale, snaps), in_specs=[fa...  16.1 us
    all_to_all x3, starting transfers between devices, swap(): return lax.all_to_all(value, axes, split_axis=0, concat_axis=0, tiled=True)  12.8 us
    all_to_all x1, blocking collectives, swap(): return lax.all_to_all(value, axes, split_axis=0, concat_axis=0, tiled=True)  11.6 us
    all_to_all x3, waiting for transfers between devices, swap(): return lax.all_to_all(value, axes, split_axis=0, concat_axis=0, tiled=True)  9.7 us
    pallas_call x1, Pallas kernels, outer(): pl.pallas_call(outer_kernel, grid=(units // chunk,), in_specs=[pl.BlockSp...  8.05 us
    pallas_call x2, Pallas kernels, by_row(): pl.pallas_call(functools.partial(by_row_kernel, half * units), in_specs=[...  7.36 us
    ppermute x1, starting transfers between devices, per_device(): top = lax.ppermute(own, 'strip', down)  3.8 us
    pallas_call x1, Pallas kernels, backward(): pl.pallas_call(backward_kernel, in_specs=[far] * 6, out_specs=[far] * 3,...  3.27 us
  transfers between devices with their start and end apart: 5, of which 3 were waited for; matrix products, arithmetic and copies ran while one was open for 0% of the time, Pallas kernels for 20%

profile of v6, /device:TPU:0, one launch (start us, length us, event | category | flops | bytes accessed | tf_op | source)
XLA Modules:
  0.0 78.2 jit_solution(8744563381886610594)
XLA Ops:
  1.3 2.9 %shard_map.129 = (f32[4,2,32,384]{3,2,1,0:T(8,128)}, f32[32,8,128]{2,1,0:T(8,128)}) custom-call(s32[1]{0:T(128)S(6)} %copy.14.count_ref, s32[1,16]{1,0:T(1,128)} %emit_ref.1, f32[1,32,1024]{2,1,0:T(8,128)} %field_far.1, f32[1,32,1024]{2,1,0:T(8,128)} %kappa_far.1, bf16[4,128]{1,0:T(4,128)(2,1)} %inputs_far.1), custom_call_target="tpu_custom_call" | custom-call | tf_op jit(solution)/shard_map/pallas_call | solution.py:112
  4.2 5.2 %all-to-all-start = ((f32[4,2,32,384]{3,2,1,0:T(8,128)}), f32[4,2,32,384]{3,2,1,0:T(8,128)S(1)}, u32[]{:S(2)}, u32[]{:S(2)}) async-start(f32[4,2,32,384]{3,2,1,0:T(8,128)} %get-tuple-element.25), calls=%async_computation | async-start | bytes 786432 | tf_op jit(solution)/shard_map/all_to_all | solution.py:546
  9.4 3.7 %shard_map.130.low_far = bf16[32,256,256]{2,1,0:T(8,128)(2,1)} custom-call(bf16[512,32,256]{2,1,0:T(8,128)(2,1)} %weight_far.1), custom_call_target="tpu_custom_call" | custom-call | bytes 8388608 | tf_op jit(solution)/shard_map/pallas_call | solution.py:200
  13.0 3.0 %all-to-all-done.own_far = f32[4,2,32,384]{3,2,1,0:T(8,128)S(1)} async-done(((f32[4,2,32,384]{3,2,1,0:T(8,128)}), f32[4,2,32,384]{3,2,1,0:T(8,128)S(1)}, u32[]{:S(2)}, u32[]{:S(2)}) %all-to-all-start) | async-done | bytes 393248 | tf_op jit(solution)/shard_map/all_to_all | solution.py:546
  16.0 0.0 copy-start
  16.0 1.3 %collective-permute-start.1 = (f32[4,2,32,384]{3,2,1,0:T(8,128)S(1)}, f32[4,2,32,384]{3,2,1,0:T(8,128)}, u32[]{:S(2)}, u32[]{:S(2)}) collective-permute-start(f32[4,2,32,384]{3,2,1,0:T(8,128)S(1)} %all-to-all-done.own_far), channel_id=1, source_target_pairs={{1,0},{2,1},{3,2},{4,3},{5,4},{6,5},{7,6},{9,8},{10,9},{11,10},{12... | collective-permute-start | bytes 1179656 | tf_op jit(solution)/shard_map/ppermute | solution.py:574
  17.3 3.8 %collective-permute-start = (f32[4,2,32,384]{3,2,1,0:T(8,128)S(1)}, f32[4,2,32,384]{3,2,1,0:T(8,128)}, u32[]{:S(2)}, u32[]{:S(2)}) collective-permute-start(f32[4,2,32,384]{3,2,1,0:T(8,128)S(1)} %all-to-all-done.own_far), channel_id=1, source_target_pairs={{0,1},{1,2},{2,3},{3,4},{4,5},{5,6},{6,7},{8,9},{9,10},{10,11},{11... | collective-permute-start | bytes 1179656 | tf_op jit(solution)/shard_map/ppermute | solution.py:573
  21.1 5.0 %all-to-all-start.1 = ((f32[32,8,128]{2,1,0:T(8,128)}), f32[32,8,128]{2,1,0:T(8,128)}, u32[]{:S(2)}, u32[]{:S(2)}) async-start(f32[32,8,128]{2,1,0:T(8,128)} %get-tuple-element.30), calls=%async_computation.1 | async-start | bytes 262144 | tf_op jit(solution)/shard_map/all_to_all | solution.py:546
  26.1 3.7 %shard_map.131.high_far = bf16[32,256,256]{2,1,0:T(8,128)(2,1)} custom-call(bf16[512,32,256]{2,1,0:T(8,128)(2,1)} %weight_far.1), custom_call_target="tpu_custom_call" | custom-call | bytes 8388608 | tf_op jit(solution)/shard_map/pallas_call | solution.py:200
  29.8 0.0 copy-done
  29.8 4.4 %all-to-all-done.1.seed_far = f32[32,8,128]{2,1,0:T(8,128)} async-done(((f32[32,8,128]{2,1,0:T(8,128)}), f32[32,8,128]{2,1,0:T(8,128)}, u32[]{:S(2)}, u32[]{:S(2)}) %all-to-all-start.1) | async-done | bytes 131104 | tf_op jit(solution)/shard_map/all_to_all | solution.py:546
  34.2 0.0 collective-permute-done.1.bottom_far
  34.2 0.0 collective-permute-done.top_far
  34.2 16.1 %shard_map.132 = (bf16[32,128,256]{2,1,0:T(8,128)(2,1)}, f32[32,16,128]{2,1,0:T(8,128)}, bf16[128,128]{1,0:T(8,128)(2,1)}, f32[128,512]{1,0:T(8,128)}, f32[128,512]{1,0:T(8,128)}, /*index=5*/bf16[128,512]{1,0:T(8,128)(2,1)}) custom-call(f32[4,2,32,384]{3,2,1,0:T(8,128)} %copy-done, f32[4,2,32,384]{3,2,1,0:T(8,128)} %collective-permute-done.top_far, ...), custom_call_target="tpu_custom_call" | custom-call | tf_op jit(solution)/shard_map/pallas_call | solution.py:384
  50.3 2.6 %all-to-all-start.2 = ((f32[32,16,128]{2,1,0:T(8,128)}), f32[32,16,128]{2,1,0:T(8,128)S(1)}, u32[]{:S(2)}, u32[]{:S(2)}) async-start(f32[32,16,128]{2,1,0:T(8,128)} %get-tuple-element.36), calls=%async_computation.2 | async-start | bytes 524288 | tf_op jit(solution)/shard_map/all_to_all | solution.py:546
  52.9 8.1 %shard_map.133 = bf16[512,32,256]{2,1,0:T(8,128)(2,1)} custom-call(bf16[128,512]{1,0:T(8,128)(2,1)} %get-tuple-element.37.hid_ref, bf16[32,128,256]{2,1,0:T(8,128)(2,1)} %get-tuple-element.38.res_ref), custom_call_target="tpu_custom_call" | custom-call | flops 1073741824 | bytes 16777216 | tf_op jit(solution)/shard_map/pallas_call | solution.py:434
  61.0 2.3 %all-to-all-done.2.pieces = f32[32,16,128]{2,1,0:T(8,128)S(1)} async-done(((f32[32,16,128]{2,1,0:T(8,128)}), f32[32,16,128]{2,1,0:T(8,128)S(1)}, u32[]{:S(2)}, u32[]{:S(2)}) %all-to-all-start.2) | async-done | bytes 262176 | tf_op jit(solution)/shard_map/all_to_all | solution.py:546
  63.4 11.6 %all_to_all.20.delta_far = bf16[32,16,128]{2,1,0:T(8,128)(2,1)} all-to-all(bf16[32,16,128]{2,1,0:T(8,128)(2,1)S(1)} %shard_map.134), channel_id=1, replica_groups=mesh['group'=4,'strip'=8] {'group','strip'}, dimensions={0} | all-to-all | bytes 262144 | tf_op jit(solution)/shard_map/all_to_all | solution.py:546
  75.0 3.3 %shard_map.135 = (f32[128,512]{1,0:T(8,128)}, f32[512,512]{1,0:T(8,128)}, f32[512,512]{1,0:T(8,128)}) custom-call(bf16[128,128]{1,0:T(8,128)(2,1)} %get-tuple-element.33.inputs_far, f32[128,512]{1,0:T(8,128)} %get-tuple-element.34.a_far, f32[128,512]{1,0:T(8,128)} %get-tuple-element.35.b_far, bf16[32,16,128]{2,1,0:T(8,128)(2,1)} %all_to_all.20.delta_far, ...), custom_call_target="tpu_custom_call" | custom-call | tf_op jit(solution)/shard_map/pallas_call | solution.py:524
  (1 shorter events, 0.0 us)
Async XLA Ops:
  4.2 11.8 %all-to-all-start = ((f32[4,2,32,384]{3,2,1,0:T(8,128)}), f32[4,2,32,384]{3,2,1,0:T(8,128)S(1)}, u32[]{:S(2)}, u32[]{:S(2)}) async-start(f32[4,2,32,384]{3,2,1,0:T(8,128)} %get-tuple-element.25), calls=%async_computation | async-start | bytes 786432 | tf_op jit(solution)/shard_map/all_to_all | solution.py:546
  16.0 13.8 %copy-start = (f32[4,2,32,384]{3,2,1,0:T(8,128)}, f32[4,2,32,384]{3,2,1,0:T(8,128)S(1)}, u32[]{:S(2)}) copy-start(f32[4,2,32,384]{3,2,1,0:T(8,128)S(1)} %all-to-all-done.own_far) | copy-start | bytes 1179652
  16.0 18.2 %collective-permute-start.1 = (f32[4,2,32,384]{3,2,1,0:T(8,128)S(1)}, f32[4,2,32,384]{3,2,1,0:T(8,128)}, u32[]{:S(2)}, u32[]{:S(2)}) collective-permute-start(f32[4,2,32,384]{3,2,1,0:T(8,128)S(1)} %all-to-all-done.own_far), channel_id=1, source_target_pairs={{1,0},{2,1},{3,2},{4,3},{5,4},{6,5},{7,6},{9,8},{10,9},{11,10},{12... | collective-permute-start | bytes 1179656 | tf_op jit(solution)/shard_map/ppermute | solution.py:574
  17.3 17.0 %collective-permute-start = (f32[4,2,32,384]{3,2,1,0:T(8,128)S(1)}, f32[4,2,32,384]{3,2,1,0:T(8,128)}, u32[]{:S(2)}, u32[]{:S(2)}) collective-permute-start(f32[4,2,32,384]{3,2,1,0:T(8,128)S(1)} %all-to-all-done.own_far), channel_id=1, source_target_pairs={{0,1},{1,2},{2,3},{3,4},{4,5},{5,6},{6,7},{8,9},{9,10},{10,11},{11... | collective-permute-start | bytes 1179656 | tf_op jit(solution)/shard_map/ppermute | solution.py:573
  21.1 13.1 %all-to-all-start.1 = ((f32[32,8,128]{2,1,0:T(8,128)}), f32[32,8,128]{2,1,0:T(8,128)}, u32[]{:S(2)}, u32[]{:S(2)}) async-start(f32[32,8,128]{2,1,0:T(8,128)} %get-tuple-element.30), calls=%async_computation.1 | async-start | bytes 262144 | tf_op jit(solution)/shard_map/all_to_all | solution.py:546
  50.3 13.0 %all-to-all-start.2 = ((f32[32,16,128]{2,1,0:T(8,128)}), f32[32,16,128]{2,1,0:T(8,128)S(1)}, u32[]{:S(2)}, u32[]{:S(2)}) async-start(f32[32,16,128]{2,1,0:T(8,128)} %get-tuple-element.36), calls=%async_computation.2 | async-start | bytes 524288 | tf_op jit(solution)/shard_map/all_to_all | solution.py:546
